TPU v7x, 32 devices: a whole 2x2x4 slice. The times are simulated.
32 devices in a mesh: dp: 8 (over z, core), ctx: 4 (over y, x).
Axes of the slice: x: 2, y: 2, z: 4, core: 2. Of those that a mesh axis runs over, the one named last changes fastest.
Arguments:
- actions: bfloat16 [8, 512, 1024], P('dp', 'ctx'), may hold values from -6 to 6
- stamps: int32 [8, 512], P('dp', 'ctx'), may hold values from 0 to 65408, as said below
- lengths: int32 [8], P('dp'), may hold values from 128 to 512, as said below
- w_proj: bfloat16 [1024, 1024], replicated, may hold values from -0.1875 to 0.1875
- w_out: bfloat16 [256, 1024], replicated, may hold values from -0.375 to 0.375
- bias_table: float32 [16, 4], replicated, may hold values from -4 to 4
- grad_out: bfloat16 [8, 512, 1024], P('dp', 'ctx'), may hold values from -6 to 6
Outputs:
- layer_out: bfloat16 [8, 512, 1024], P('dp', 'ctx')
- grad_actions: bfloat16 [8, 512, 1024], P('dp', 'ctx')
- grad_table: float32 [16, 4], replicated
Inputs may be any that keep to these rules, and one draw needn't show every extreme that they name: lengths 512 and 128 occur in every draw. `stamps`: non-decreasing along each row from 0, by steps of 1 to 128.
All inputs are finite; a program needn't handle non-finite values.
Results may differ from a plain program's by a relative error of at most 0.0077.
Values may be sent and summed in bfloat16 or wider, within the bound.
A program may use at most 64 MiB of HBM per device.

v0:
```python
import math

import jax
import jax.numpy as jnp
from jax import lax
from jax.sharding import PartitionSpec as P

EPS = 1e-05


def norm_rows(values):
    row_mean = jnp.mean(values, axis=-1, keepdims=True)
    centred = values - row_mean
    spread = jnp.mean(centred * centred, axis=-1, keepdims=True)
    inverse = lax.rsqrt(spread + EPS)
    return (centred * inverse, inverse)


def norm_back(incoming, normed, inverse):
    first = jnp.mean(incoming, axis=-1, keepdims=True)
    second = jnp.mean(incoming * normed, axis=-1, keepdims=True)
    return inverse * (incoming - first - normed * second)


def silu_slope(values):
    sigmoid_val = jax.nn.sigmoid(values)
    return sigmoid_val * (1.0 + values * (1.0 - sigmoid_val))


def block_bias(stamp_gap, table_vals):
    bias_sum = (
        jnp.zeros((table_vals.shape[1],) + stamp_gap.shape, jnp.float32)
        + table_vals[0][:, None, None]
    )
    for level_index in range(table_vals.shape[0] - 1):
        above_level = (stamp_gap >= 1 << level_index).astype(jnp.float32)
        bias_sum = (
            bias_sum
            + above_level[None]
            * (table_vals[level_index + 1] - table_vals[level_index])[:, None, None]
        )
    return bias_sum


def gap_buckets(stamp_gap, level_count):
    found = jnp.zeros(stamp_gap.shape, jnp.int32)
    for level_index in range(level_count - 1):
        found = found + (stamp_gap >= 1 << level_index).astype(jnp.int32)
    return found


def table_terms(grad_scores, buckets, level_count):
    rows = [
        jnp.sum(jnp.where(buckets[None] == level_index, grad_scores, 0.0), axis=(1, 2))
        for level_index in range(level_count)
    ]
    return jnp.stack(rows, axis=0)


def on_device(actions, stamps, lengths, w_proj, w_out, bias_table, grad_out):
    tok_rows = actions.shape[1]
    model_dim = actions.shape[2]
    level_count = bias_table.shape[0]
    head_count = bias_table.shape[1]
    attn_dim = w_out.shape[0]
    head_dim = attn_dim // head_count
    ctx_count = lax.axis_size("ctx")
    data_count = lax.axis_size("dp")
    ctx_rank = lax.axis_index("ctx")
    hist_rows = tok_rows * ctx_count
    block_rows = min(512, hist_rows)
    block_count = hist_rows // block_rows
    length = lengths[0]
    inputs = actions.reshape(tok_rows, model_dim)
    own_stamps = stamps.reshape(tok_rows)
    upstream = grad_out.reshape(tok_rows, model_dim)
    score_scale = head_dim ** (-0.5)
    normed, inverse = norm_rows(inputs.astype(jnp.float32))
    pre_act = jnp.dot(normed.astype(jnp.bfloat16), w_proj, preferred_element_type=jnp.float32)
    activated = jax.nn.silu(pre_act).astype(jnp.bfloat16)
    gate_units = activated[:, :attn_dim].astype(jnp.float32)
    queries = activated[:, attn_dim : 2 * attn_dim]
    own_keys = activated[:, 2 * attn_dim : 3 * attn_dim]
    own_values = activated[:, 3 * attn_dim :]
    all_kv, all_stamps = (
        lax.all_gather(activated[:, 2 * attn_dim :], "ctx", axis=0, tiled=True),
        lax.all_gather(own_stamps, "ctx", axis=0, tiled=True),
    )
    all_keys = all_kv[:, :attn_dim]
    all_values = all_kv[:, attn_dim:]
    own_pos = ctx_rank * tok_rows + jnp.arange(tok_rows, dtype=jnp.int32)
    counts = (jnp.minimum(own_pos, length - 1) + 1).astype(jnp.float32)
    query_heads = queries.reshape(tok_rows, head_count, head_dim)
    query_first = 0

    def key_block(block_index):
        start = block_index * block_rows
        key_rows = lax.dynamic_slice_in_dim(all_keys, start, block_rows, 0).reshape(
            block_rows, head_count, head_dim
        )
        value_rows = lax.dynamic_slice_in_dim(all_values, start, block_rows, 0).reshape(
            block_rows, head_count, head_dim
        )
        key_stamps = lax.dynamic_slice_in_dim(all_stamps, start, block_rows, 0)
        key_pos = start + jnp.arange(block_rows, dtype=jnp.int32)
        visible = (key_pos[None, :] <= own_pos[:, None]) & (key_pos[None, :] < length)
        stamp_gap = own_stamps[:, None] - key_stamps[None, :]
        scores = jnp.einsum(
            "qhd,khd->hqk", query_heads, key_rows, preferred_element_type=jnp.float32
        ) * score_scale + block_bias(stamp_gap, bias_table)
        return (key_rows, value_rows, visible, stamp_gap, scores)

    def forward_step(block_index, mixed_acc):
        key_rows, value_rows, visible, stamp_gap, scores = key_block(block_index)
        weights = (
            jnp.where(visible[None], jax.nn.silu(scores), 0.0) / counts[None, :, None]
        ).astype(jnp.bfloat16)
        return mixed_acc + jnp.einsum(
            "hqk,khd->qhd", weights, value_rows, preferred_element_type=jnp.float32
        )

    mixed_sum = lax.fori_loop(
        0, block_count, forward_step, jnp.zeros((tok_rows, head_count, head_dim), jnp.float32)
    )
    mixed_out = mixed_sum.reshape(tok_rows, attn_dim)
    mixed_norm, mixed_inv = norm_rows(mixed_out)
    gated_rows = (mixed_norm * gate_units).astype(jnp.bfloat16)
    layer_rows = (
        inputs.astype(jnp.float32) + jnp.dot(gated_rows, w_out, preferred_element_type=jnp.float32)
    ).astype(jnp.bfloat16)
    grad_gated = jnp.dot(upstream, w_out.T, preferred_element_type=jnp.float32)
    grad_units = grad_gated * mixed_norm
    grad_mixed = norm_back(grad_gated * gate_units, mixed_norm, mixed_inv).astype(jnp.bfloat16)
    grad_heads = grad_mixed.reshape(tok_rows, head_count, head_dim)

    def query_back_step(block_index, carry):
        grad_q_acc, table_acc = carry
        key_rows, value_rows, visible, stamp_gap, scores = key_block(block_index)
        grad_weights = jnp.einsum(
            "qhd,khd->hqk", grad_heads, value_rows, preferred_element_type=jnp.float32
        )
        grad_scores = (
            jnp.where(visible[None], grad_weights * silu_slope(scores), 0.0) / counts[None, :, None]
        ).astype(jnp.bfloat16)
        grad_q_acc = grad_q_acc + jnp.einsum(
            "hqk,khd->qhd", grad_scores, key_rows, preferred_element_type=jnp.float32
        )
        table_acc = table_acc + table_terms(
            grad_scores.astype(jnp.float32), gap_buckets(stamp_gap, level_count), level_count
        )
        return (grad_q_acc, table_acc)

    query_start = (
        jnp.zeros((tok_rows, head_count, head_dim), jnp.float32),
        jnp.zeros((level_count, head_count), jnp.float32),
    )
    grad_q_sum, table_local = lax.fori_loop(0, block_count, query_back_step, query_start)
    grad_queries = grad_q_sum.reshape(tok_rows, attn_dim) * score_scale
    all_queries, all_grads = (
        lax.all_gather(queries, "ctx", axis=0, tiled=True),
        lax.all_gather(grad_mixed, "ctx", axis=0, tiled=True),
    )
    own_key_heads = own_keys.reshape(tok_rows, head_count, head_dim)
    own_value_heads = own_values.reshape(tok_rows, head_count, head_dim)

    def key_back_step(block_index, carry):
        grad_k_acc, grad_v_acc = carry
        start = block_index * block_rows
        block_queries = lax.dynamic_slice_in_dim(all_queries, start, block_rows, 0).reshape(
            block_rows, head_count, head_dim
        )
        block_grads = lax.dynamic_slice_in_dim(all_grads, start, block_rows, 0).reshape(
            block_rows, head_count, head_dim
        )
        block_stamps = lax.dynamic_slice_in_dim(all_stamps, start, block_rows, 0)
        block_pos = start + jnp.arange(block_rows, dtype=jnp.int32)
        block_counts = (jnp.minimum(block_pos, length - 1) + 1).astype(jnp.float32)
        seen_by = (own_pos[None, :] <= block_pos[:, None]) & (own_pos[None, :] < length)
        stamp_gap = block_stamps[:, None] - own_stamps[None, :]
        scores = jnp.einsum(
            "qhd,khd->hqk", block_queries, own_key_heads, preferred_element_type=jnp.float32
        ) * score_scale + block_bias(stamp_gap, bias_table)
        weights = (
            jnp.where(seen_by[None], jax.nn.silu(scores), 0.0) / block_counts[None, :, None]
        ).astype(jnp.bfloat16)
        grad_v_acc = grad_v_acc + jnp.einsum(
            "hqk,qhd->khd", weights, block_grads, preferred_element_type=jnp.float32
        )
        grad_weights = jnp.einsum(
            "qhd,khd->hqk", block_grads, own_value_heads, preferred_element_type=jnp.float32
        )
        grad_scores = (
            jnp.where(seen_by[None], grad_weights * silu_slope(scores), 0.0)
            / block_counts[None, :, None]
        ).astype(jnp.bfloat16)
        grad_k_acc = grad_k_acc + jnp.einsum(
            "hqk,qhd->khd", grad_scores, block_queries, preferred_element_type=jnp.float32
        )
        return (grad_k_acc, grad_v_acc)

    key_start = (
        jnp.zeros((tok_rows, head_count, head_dim), jnp.float32),
        jnp.zeros((tok_rows, head_count, head_dim), jnp.float32),
    )
    grad_k_sum, grad_v_sum = lax.fori_loop(query_first, block_count, key_back_step, key_start)
    grad_keys = grad_k_sum.reshape(tok_rows, attn_dim) * score_scale
    grad_values = grad_v_sum.reshape(tok_rows, attn_dim)
    grad_act = jnp.concatenate([grad_units, grad_queries, grad_keys, grad_values], axis=1)
    grad_pre = (grad_act * silu_slope(pre_act)).astype(jnp.bfloat16)
    grad_normed = jnp.dot(grad_pre, w_proj.T, preferred_element_type=jnp.float32)
    grad_rows = (norm_back(grad_normed, normed, inverse) + upstream.astype(jnp.float32)).astype(
        jnp.bfloat16
    )
    table_total = lax.psum(table_local, ("dp", "ctx"))
    grad_table = table_total * (1.0 / math.sqrt(hist_rows * data_count))
    return (
        layer_rows.reshape(1, tok_rows, model_dim),
        grad_rows.reshape(1, tok_rows, model_dim),
        grad_table,
    )


def solution(mesh):
    in_specs = (P("dp", "ctx", None), P("dp", "ctx"), P("dp"), P(), P(), P(), P("dp", "ctx", None))
    out_specs = (P("dp", "ctx", None), P("dp", "ctx", None), P())
    return jax.shard_map(
        on_device, mesh=mesh, in_specs=in_specs, out_specs=out_specs, check_vma=False
    )
```

profile of v0, /device:TPU:0, one launch (start us, length us, event | category | flops | bytes accessed | tf_op | source)
XLA Modules:
  0.0 159.8 jit_solution(16327815124184986514)
XLA Ops:
  0.6 0.0 copy-start
  0.6 1.7 %slice_reduce_fusion.15 = (f32[4]{0:T(128)S(1)}, f32[4]{0:T(128)S(1)}, f32[4]{0:T(128)S(1)}, f32[4]{0:T(128)S(1)}, f32[4]{0:T(128)S(1)}, /*index=5*/f32[4]{0:T(1...) fusion(f32[16,4]{0,1:T(4,128)} %param.12), kind=kLoop, calls=%fused_computation.229 | loop fusion | bytes 512 | tf_op jit(solution)/shard_map/while/body/eval_jaxpr/slice | solution.py:33
  2.4 0.7 fusion.142
  3.1 9.5 %all-gather = s32[1,512]{1,0:T(1,128)S(1)} all-gather(s32[1,128]{1,0:T(1,128)} %param.8), channel_id=2, replica_groups=mesh['dp'=8,'ctx'=4] {'ctx'}, dimensions={1}, use_global_device_ids=true | all-gather | bytes 2560 | tf_op jit(solution)/shard_map/all_gather | solution.py:87
  12.5 3.6 %broadcast_compare_fusion.11 = (pred[128,512]{1,0:T(8,128)(4,1)}, pred[128,512]{1,0:T(8,128)(4,1)}, pred[128,512]{1,0:T(8,128)(4,1)}, pred[128,512]{1,0:T(8,128)...) fusion(s32[512]{0:T(512)S(1)} %bitcast.123, ...), kind=kLoop, calls=%fused_computation.200 | loop fusion | flops 4980736 | bytes 4983296 | tf_op jit(solution)/shard_map/while/body/eval_jaxpr/eq | solution.py:54
  16.2 0.1 convert_reduce_fusion
  16.3 0.2 fusion.43
  16.5 1.3 multiply_convert_fusion
  17.8 0.7 fusion.141
  18.6 0.7 copy.39
  19.3 10.5 %all_gather.12 = bf16[512,512]{1,0:T(8,128)(2,1)S(1)} all-gather(bf16[128,512]{1,0:T(8,128)(2,1)S(1)} %slice.217), channel_id=1, replica_groups=mesh['dp'=8,'ctx'=4] {'ctx'}, dimensions={0}, use_global_device_ids=true | all-gather | bytes 655360 | tf_op jit(solution)/shard_map/all_gather | solution.py:86
  29.8 0.7 fusion.140
  30.5 1.1 copy.40
  31.6 4.5 %fusion.5 = f32[4,128,512]{2,1,0:T(8,128)} fusion(bf16[128,4,64]{0,2,1:T(8,128)(2,1)} %bitcast.121, bf16[512,4,64]{0,2,1:T(8,128)(2,1)S(1)} %bitcast.107, f32[4]{0:T(128)} %get-tuple-element.229, f32[128,512]{1,0:T(8,128)} %get-tuple-element.185, f32[4]{0:T(128)} %get-tuple-element.228, f32[128,512]{1,0:T(8,128)} %get-tuple-element.186, ...), kind=kOutput, calls=%fused_computation.55 | convolution fusion | flops 41943040 | bytes 5308672 | tf_op jit(solution)/shard_map/while/body/eval_jaxpr/qhd,khd->hqk/dot_general | solution.py:108
  36.1 0.8 copy.38
  37.6 0.7 fusion.105
  38.3 0.0 copy-start.2
  38.4 0.0 copy-start.3
  38.4 1.8 %fusion.143 = (f32[128]{0:T(128)S(1)}, f32[4,64,128]{2,1,0:T(8,128)S(1)}) fusion(bf16[512,4,64]{0,2,1:T(8,128)(2,1)} %bitcast.111, f32[4,128,512]{2,1,0:T(8,128)} %fusion.5, f32[128]{0:T(128)S(1)} %add_convert_fusion.1, pred[128,512]{1,0:T(8,128)(4,1)} %fusion.105), kind=kOutput, calls=%fused_computation.255 | convolution fusion | flops 35422080 | bytes 1508352 | tf_op jit(solution)/shard_map/while/body/eval_jaxpr/hqk,khd->qhd/dot_general | solution.py:118
  40.2 0.0 copy-start.7
  40.3 0.1 fusion.124
  40.3 0.6 copy-done.7
  40.9 1.0 copy.41
  41.9 1.2 fusion.130
  43.2 1.6 %fusion.125 = (f32[128,256]{1,0:T(8,128)}, bf16[128,256]{1,0:T(8,128)(2,1)}) fusion(f32[128,256]{1,0:T(8,128)S(1)} %get-tuple-element.234, f32[128,256]{1,0:T(8,128)S(1)} %copy.41, f32[128]{0:T(128)S(1)} %add_rsqrt_fusion, f32[128]{0:T(128)S(1)} %broadcast_multiply_fusion.3, f32[128]{0:T(128)S(1)} %get-tuple-element.237, f32[128]{0:T(128)S(1)} %get-tuple-element.238, ...), kind=kLoop, calls=%fused_computation.208 | loop fusion | flops 327680 | bytes 526336 | tf_op jit(solution)/shard_map/mul | solution.py:132
  44.8 1.6 copy.42
  46.4 5.1 %fusion.27 = (f32[4]{0:T(128)}, f32[4]{0:T(128)S(1)}, f32[4]{0:T(128)}, f32[4]{0:T(128)}, f32[4]{0:T(128)}, /*index=5*/f32[4]{0:T(128)}, f32[4]{0:T(128)}, f32[4...) fusion(pred[128,512]{1,0:T(8,128)(4,1)} %get-tuple-element.184,, ...), kind=kOutput, calls=%fused_computation.79 | convolution fusion | flops 45088704 | bytes 3015424 | tf_op jit(solution)/shard_map/while/body/eval_jaxpr/qhd,khd->hqk/dot_general | solution.py:139
  51.4 0.7 copy.50
  52.1 0.1 copy.51
  52.2 0.7 copy.52
  52.9 1.3 copy.53
  54.3 1.3 copy.54
  55.6 1.2 copy.55
  56.8 1.3 copy.56
  58.1 1.3 copy.57
  59.4 1.3 copy.58
  60.7 1.3 copy.59
  61.9 1.2 copy.60
  63.2 1.3 copy.61
  64.5 1.3 copy.62
  65.8 1.3 copy.63
  67.1 1.3 copy.64
  68.4 1.3 copy.65
  69.7 1.5 stack.84
  71.1 39.8 %psum.7 = f32[16,4]{0,1:T(4,128)S(1)} all-reduce(f32[16,4]{0,1:T(4,128)} %stack.84), channel_id=1, replica_groups=mesh['dp'=8,'ctx'=4] {'dp','ctx'}, use_global_device_ids=true, to_apply=%region_24.25 | all-reduce | flops 64 | bytes 512 | tf_op jit(solution)/shard_map/psum | solution.py:214
  110.9 0.6 broadcast_multiply_fusion
  111.5 2.0 %convolution_multiply_fusion.4 = f32[4,64,128]{2,1,0:T(8,128)} fusion(bf16[512,4,64]{0,2,1:T(8,128)(2,1)S(1)} %bitcast.108, bf16[4,128,512]{2,1,0:T(8,128)(2,1)} %get-tuple-element.236), kind=kOutput, calls=%fused_computation.62 | convolution fusion | flops 33587200 | bytes 917504 | tf_op jit(solution)/shard_map/while/body/eval_jaxpr/hqk,khd->qhd/dot_general | solution.py:145
  113.5 1.6 %copy.47 = f32[128,256]{1,0:T(8,128)} copy(f32[128,256]{0,1:T(8,128)} %bitcast.109) | data formatting | bytes 262144 | tf_op jit(solution)/shard_map/mul | solution.py:158
  115.1 10.2 %all_gather.14 = bf16[512,256]{1,0:T(8,128)(2,1)S(1)} all-gather(bf16[128,256]{1,0:T(8,128)(2,1)} %copy-done.5), channel_id=1, replica_groups=mesh['dp'=8,'ctx'=4] {'ctx'}, dimensions={0}, use_global_device_ids=true | all-gather | bytes 327680 | tf_op jit(solution)/shard_map/all_gather | solution.py:160
  125.3 0.8 copy.43
  126.1 3.1 %fusion.107 = (f32[512,128]{1,0:T(8,128)}, f32[512,128]{1,0:T(8,128)}, f32[512,128]{1,0:T(8,128)}, f32[512,128]{1,0:T(8,128)}, f32[512,128]{1,0:T(8,128)}, /*ind...) fusion(s32[128]{0:T(128)} %bitcast.126, ...), kind=kLoop, calls=%fused_computation.168 | loop fusion | flops 2031616 | bytes 3934720 | tf_op jit(solution)/shard_map/while/body/eval_jaxpr/convert_element_type | solution.py:36
  129.2 1.6 copy.46
  130.8 4.6 %fusion = f32[4,512,128]{2,1,0:T(8,128)} fusion(bf16[512,4,64]{0,2,1:T(8,128)(2,1)S(1)} %bitcast.114, bf16[128,4,64]{0,2,1:T(8,128)(2,1)} %bitcast.120, f32[4]{0:T(128)} %get-tuple-element.229, f32[512,128]{1,0:T(8,128)} %get-tuple-element.201, f32[4]{0:T(128)} %get-tuple-element.228, f32[512,128]{1,0:T(8,128)} %get-tuple-element.202, ...), kind=kOutput, calls=%fused_computation.47 | convolution fusion | flops 41943040 | bytes 5308672 | tf_op jit(solution)/shard_map/while/body/eval_jaxpr/qhd,khd->hqk/dot_general | solution.py:180
  135.4 8.4 %all_gather.15 = bf16[512,256]{1,0:T(8,128)(2,1)S(1)} all-gather(bf16[128,256]{1,0:T(8,128)(2,1)S(1)} %copy-done.6), channel_id=1, replica_groups=mesh['dp'=8,'ctx'=4] {'ctx'}, dimensions={0}, use_global_device_ids=true | all-gather | bytes 327680 | tf_op jit(solution)/shard_map/all_gather | solution.py:161
  143.8 0.8 copy.44
  144.6 1.6 copy.45
  146.2 0.7 fusion.106
  146.9 2.8 %fusion.11 = f32[4,64,128]{2,1,0:T(8,128)} fusion(bf16[512,4,64]{0,2,1:T(8,128)(2,1)} %bitcast.113, bf16[512,4,64]{0,2,1:T(8,128)(2,1)} %bitcast.115, bf16[128,4,64]{0,2,1:T(8,128)(2,1)} %bitcast.122, f32[4,512,128]{2,1,0:T(8,128)} %fusion, f32[512]{0:T(512)S(1)} %add_convert_fusion, pred[512,128]{1,0:T(8,128)(4,1)} %fusion.106), kind=kOutput, calls=%fused_computation.63 | convolution fusion | flops 70025216 | bytes 1837056 | tf_op jit(solution)/shard_map/while/body/eval_jaxpr/hqk,qhd->khd/dot_general | solution.py:196
  149.7 1.7 %copy.48 = f32[128,256]{1,0:T(8,128)} copy(f32[128,256]{0,1:T(8,128)} %bitcast.118) | data formatting | bytes 262144 | tf_op jit(solution)/shard_map/mul | solution.py:206
  151.4 2.4 %fusion.50 = f32[4,64,128]{2,1,0:T(8,128)} fusion(bf16[512,4,64]{0,2,1:T(8,128)(2,1)S(1)} %bitcast.116, f32[4,512,128]{2,1,0:T(8,128)} %fusion, f32[512]{0:T(512)S(1)} %add_convert_fusion, pred[512,128]{1,0:T(8,128)(4,1)} %fusion.106), kind=kOutput, calls=%fused_computation.111 | convolution fusion | flops 35389440 | bytes 1509376 | tf_op jit(solution)/shard_map/while/body/eval_jaxpr/hqk,qhd->khd/dot_general | solution.py:186
  153.8 1.0 copy.49
  154.8 2.2 %fusion.139 = (f32[128]{0:T(128)S(1)}, f32[128]{0:T(128)S(1)}, f32[128,1024]{1,0:T(8,128)S(1)}) fusion(f32[128]{0:T(128)S(1)} %copy-done.21, f32[128]{0:T(128)S(1)} %copy-done.15, bf16[1,128,1024]{2,1,0:T(8,128)(2,1)S(1)} %copy-done.1, bf16[1024,1024]{1,0:T(8,128)(2,1)S(1)} %copy-done, f32[128,256]{1,0:T(8,128)S(1)} %copy.49, f32[128,256]{1,0:T(8,128)} %copy.48, ...), kind=kOutput, calls=%fused_computation.251 | convolution fusion | flops 270794496 | bytes 3934208 | tf_op jit(solution)/shard_map/dot_general | solution.py:210
  157.0 1.0 fusion.97
  158.0 1.8 %fusion.10 = bf16[1,128,1024]{2,1,0:T(8,128)(2,1)} fusion(bf16[256,1024]{1,0:T(8,128)(2,1)S(1)} %copy-done.2, bf16[1,128,1024]{2,1,0:T(8,128)(2,1)S(1)} %copy-done.1, f32[128,256]{1,0:T(8,128)S(1)} %copy.41, f32[128]{0:T(128)S(1)} %copy-done.13, f32[128]{0:T(128)S(1)} %copy-done.11, bf16[128,1024]{1,0:T(8,128)(2,1)} %copy-done.4), kind=kOutput, calls=%fused_computation.61 | convolution fusion | flops 67665920 | bytes 1246208 | tf_op jit(solution)/shard_map/dot_general | solution.py:129
  (62 shorter events, 0.2 us)
Async XLA Ops:
  0.6 15.9 %copy-start = (bf16[1024,1024]{1,0:T(8,128)(2,1)S(1)}, bf16[1024,1024]{1,0:T(8,128)(2,1)}, u32[]{:S(2)}) copy-start(bf16[1024,1024]{1,0:T(8,128)(2,1)} %param.10) | copy-start | bytes 6291460
  2.4 29.2 %copy-start.18 = (f32[4]{0:T(128)}, f32[4]{0:T(128)S(1)}, u32[]{:S(2)}) copy-start(f32[4]{0:T(128)S(1)} %get-tuple-element.133) | copy-start | bytes 52
  3.0 28.6 %copy-start.22 = (f32[4]{0:T(128)}, f32[4]{0:T(128)S(1)}, u32[]{:S(2)}) copy-start(f32[4]{0:T(128)S(1)} %get-tuple-element.215) | copy-start | bytes 52
  3.1 28.6 %copy-start.24 = (f32[4]{0:T(128)}, f32[4]{0:T(128)S(1)}, u32[]{:S(2)}) copy-start(f32[4]{0:T(128)S(1)} %get-tuple-element.216) | copy-start | bytes 52
  12.5 3.6 %copy-start.1 = (bf16[1,128,1024]{2,1,0:T(8,128)(2,1)S(1)}, bf16[1,128,1024]{2,1,0:T(8,128)(2,1)}, u32[]{:S(2)}) copy-start(bf16[1,128,1024]{2,1,0:T(8,128)(2,1)} %param.7) | copy-start | bytes 786436
  16.3 1.6 copy-start.14
  16.5 1.3 copy-start.20
  17.8 1.4 copy-start.4
  18.6 0.7 copy-start.5
  36.9 1.4 copy-start.16
  38.3 1.9 %copy-start.26 = (f32[128]{0:T(128)}, f32[128]{0:T(128)S(1)}, u32[]{:S(2)}) copy-start(f32[128]{0:T(128)S(1)} %add_convert_fusion.1) | copy-start | bytes 1540
  38.3 3.5 %copy-start.2 = (bf16[256,1024]{1,0:T(8,128)(2,1)S(1)}, bf16[256,1024]{1,0:T(8,128)(2,1)}, u32[]{:S(2)}) copy-start(bf16[256,1024]{1,0:T(8,128)(2,1)} %param.11) | copy-start | bytes 1572868
  38.4 3.5 %copy-start.3 = (bf16[1,128,1024]{2,1,0:T(8,128)(2,1)S(1)}, bf16[1,128,1024]{2,1,0:T(8,128)(2,1)}, u32[]{:S(2)}) copy-start(bf16[1,128,1024]{2,1,0:T(8,128)(2,1)} %param.13) | copy-start | bytes 786436
  40.2 0.7 copy-start.7
  40.2 11.2 %copy-start.10 = (f32[128]{0:T(128)}, f32[128]{0:T(128)S(1)}, u32[]{:S(2)}) copy-start(f32[128]{0:T(128)S(1)} %broadcast_multiply_fusion.3) | copy-start | bytes 1540
  40.9 10.6 %copy-start.12 = (f32[128]{0:T(128)}, f32[128]{0:T(128)S(1)}, u32[]{:S(2)}) copy-start(f32[128]{0:T(128)S(1)} %add_rsqrt_fusion) | copy-start | bytes 1540
  126.1 4.6 %copy-start.8 = (bf16[512,256]{0,1:T(8,128)(2,1)S(1)}, bf16[512,256]{0,1:T(8,128)(2,1)}, u32[]{:S(2)}) copy-start(bf16[512,256]{0,1:T(8,128)(2,1)} %copy.43) | copy-start | bytes 786436
  126.1 4.6 %copy-start.19 = (f32[4]{0:T(128)S(1)}, f32[4]{0:T(128)}, u32[]{:S(2)}) copy-start(f32[4]{0:T(128)} %copy-done.18) | copy-start | bytes 52
  126.1 4.6 %copy-start.23 = (f32[4]{0:T(128)S(1)}, f32[4]{0:T(128)}, u32[]{:S(2)}) copy-start(f32[4]{0:T(128)} %copy-done.22) | copy-start | bytes 52
  126.1 4.6 %copy-start.25 = (f32[4]{0:T(128)S(1)}, f32[4]{0:T(128)}, u32[]{:S(2)}) copy-start(f32[4]{0:T(128)} %copy-done.24) | copy-start | bytes 52
  130.8 4.6 %copy-start.6 = (bf16[128,256]{1,0:T(8,128)(2,1)S(1)}, bf16[128,256]{1,0:T(8,128)(2,1)}, u32[]{:S(2)}) copy-start(bf16[128,256]{1,0:T(8,128)(2,1)} %get-tuple-element.165) | copy-start | bytes 196612
  130.8 15.4 %copy-start.17 = (s32[128]{0:T(128)S(1)}, s32[128]{0:T(128)}, u32[]{:S(2)}) copy-start(s32[128]{0:T(128)} %copy-done.16) | copy-start | bytes 1540
  146.9 4.5 %copy-start.9 = (bf16[512,256]{0,1:T(8,128)(2,1)S(1)}, bf16[512,256]{0,1:T(8,128)(2,1)}, u32[]{:S(2)}) copy-start(bf16[512,256]{0,1:T(8,128)(2,1)} %copy.44) | copy-start | bytes 786436
  151.4 3.4 %copy-start.15 = (f32[128]{0:T(128)S(1)}, f32[128]{0:T(128)}, u32[]{:S(2)}) copy-start(f32[128]{0:T(128)} %copy-done.14) | copy-start | bytes 1540
  151.4 3.4 %copy-start.21 = (f32[128]{0:T(128)S(1)}, f32[128]{0:T(128)}, u32[]{:S(2)}) copy-start(f32[128]{0:T(128)} %copy-done.20) | copy-start | bytes 1540
  154.8 3.2 %copy-start.11 = (f32[128]{0:T(128)S(1)}, f32[128]{0:T(128)}, u32[]{:S(2)}) copy-start(f32[128]{0:T(128)} %copy-done.10) | copy-start | bytes 1540
  154.8 3.2 %copy-start.13 = (f32[128]{0:T(128)S(1)}, f32[128]{0:T(128)}, u32[]{:S(2)}) copy-start(f32[128]{0:T(128)} %copy-done.12) | copy-start | bytes 1540
where the time goes:
time: 161 us; the launch traced here: 160 us
  blocking collectives  78.3 us (49%)
  local copies, waits for them, and re-layouts  37.8 us (23%)
  matrix products  29.7 us (18%)
  other arithmetic  12.4 us (8%)
  between operations  1.61 us (1%)
    psum x1, blocking collectives, on_device(): table_total = lax.psum(table_local, ('dp', 'ctx'))  39.8 us
    another operation x17, local copies, waits for them, and re-layouts, table_terms(): return jnp.stack(rows, axis=0)  19.7 us
    all_gather x1, blocking collectives, on_device(): lax.all_gather(activated[:, 2 * attn_dim:], 'ctx', axis=0, tiled=True)  10.5 us
    all_gather x1, blocking collectives, on_device(): lax.all_gather(queries, 'ctx', axis=0, tiled=True)  10.2 us
    all_gather x1, blocking collectives, on_device(): lax.all_gather(own_stamps, 'ctx', axis=0, tiled=True)  9.47 us
    all_gather x1, blocking collectives, on_device(): lax.all_gather(grad_mixed, 'ctx', axis=0, tiled=True)  8.39 us
    dot_general x1, matrix products, query_back_step(): jnp.einsum('qhd,khd->hqk', grad_heads, value_rows, preferred_element_type...  5.06 us
    dot_general x1, matrix products, key_back_step(): jnp.einsum('qhd,khd->hqk', block_queries, own_key_heads, preferred_elemen...  4.6 us

commit v1 on v0

v1 whole, which is shorter than its diff:
```python
import functools
import math

import jax
import jax.numpy as jnp
from jax import lax
from jax.experimental import pallas as pl
from jax.experimental.pallas import tpu as pltpu
from jax.sharding import PartitionSpec as P

EPS = 1e-05
MESH = pl.DeviceIdType.MESH
LANES = 128
F32 = jnp.float32
BF16 = jnp.bfloat16
NT = (((1,), (1,)), ((), ()))
TN = (((0,), (0,)), ((), ()))
NN = (((1,), (0,)), ((), ()))


def mul(left, right, dims=NN):
    return lax.dot_general(left, right, dims, preferred_element_type=F32)


def sigmoid(values):
    return 0.5 * jnp.tanh(0.5 * values) + 0.5


def norm_rows(values):
    row_mean = jnp.mean(values, axis=-1, keepdims=True)
    centred = values - row_mean
    spread = jnp.mean(centred * centred, axis=-1, keepdims=True)
    inverse = lax.rsqrt(spread + EPS)
    return centred * inverse, inverse


def norm_back(incoming, normed, inverse):
    first = jnp.mean(incoming, axis=-1, keepdims=True)
    second = jnp.mean(incoming * normed, axis=-1, keepdims=True)
    return inverse * (incoming - first - normed * second)


def silu_slope(values):
    sig = sigmoid(values)
    return sig * (1.0 + values * (1.0 - sig))


def kernel(
    ctx_count, data_count, head_count, level_count, scale_table,
    len_ref, table_ref, stamps_ref, x_hbm, wp_hbm, wo_hbm, go_hbm,
    layer_hbm, grad_hbm, gt_ref,
    xv, wp, wo, go, normed_ref, pre_ref, gate_ref, kv_all, st_all, scol, steps,
    qs, gs, buckets, sc, wt, mix, dq, own, snd, rcv, tab1, tab2, tacc,
    layer_v, grad_v,
    load_sem, out_sem, st_send, st_recv, kv_send, kv_recv, d_send, d_recv,
    t1_send, t1_recv, t2_send, t2_recv,
):
    rows, model_dim = xv.shape
    att = wo.shape[0]
    head_dim = att // head_count
    per = LANES // head_dim
    groups = att // LANES
    score_scale = head_dim ** (-0.5)
    me = lax.axis_index("ctx")
    my_dp = lax.axis_index("dp")
    ctx_at = lambda rank: {"ctx": rank}
    dp_at = lambda rank: {"dp": rank}

    def remote(src, dst, send_sem, recv_sem, where):
        return pltpu.make_async_remote_copy(
            src_ref=src, dst_ref=dst, send_sem=send_sem, recv_sem=recv_sem,
            device_id=where, device_id_type=MESH,
        )

    def loop(low, high, body):
        def step(index, carry):
            body(index)
            return carry

        lax.fori_loop(low, high, step, 0)

    load_x = pltpu.make_async_copy(x_hbm, xv, load_sem.at[0])
    load_kv = pltpu.make_async_copy(
        wp_hbm.at[:, pl.ds(2 * att, 2 * att)], wp.at[:, pl.ds(2 * att, 2 * att)], load_sem.at[1]
    )
    load_uq = pltpu.make_async_copy(
        wp_hbm.at[:, pl.ds(0, 2 * att)], wp.at[:, pl.ds(0, 2 * att)], load_sem.at[2]
    )
    load_go = pltpu.make_async_copy(go_hbm, go, load_sem.at[3])
    load_wo = pltpu.make_async_copy(wo_hbm, wo, load_sem.at[4])
    for load in (load_x, load_kv, load_uq, load_go, load_wo):
        load.start()

    barrier = pltpu.get_barrier_semaphore()
    ctx_peer = lambda offset: lax.rem(me + offset, ctx_count)
    dp_peer = lambda offset: lax.rem(my_dp + offset, data_count)

    @functools.partial(loop, 1, ctx_count)
    def _(offset):
        pl.semaphore_signal(
            barrier, inc=1, device_id=ctx_at(ctx_peer(offset)), device_id_type=MESH
        )

    @functools.partial(loop, 1, data_count)
    def _(offset):
        pl.semaphore_signal(
            barrier, inc=1, device_id=dp_at(dp_peer(offset)), device_id_type=MESH
        )

    length = len_ref[0]
    for head in range(head_count):
        running = table_ref[0, head]
        steps[0, head] = running
        for level in range(level_count - 1):
            running = running + (table_ref[level + 1, head] - table_ref[level, head])
            steps[level + 1, head] = running

    stamp_row = stamps_ref[...]
    st_all[me] = jnp.broadcast_to(stamp_row, (8, LANES))
    scol[...] = jnp.broadcast_to(stamp_row, (rows, LANES)).T

    load_x.wait()
    normed, inverse = norm_rows(xv[...].astype(F32))
    normed_ref[...] = normed
    rounded = normed.astype(BF16)
    load_kv.wait()
    pre_kv = mul(rounded, wp[:, 2 * att :])
    pre_ref[:, 2 * att :] = pre_kv
    kv_all[me] = (pre_kv * sigmoid(pre_kv)).astype(BF16)

    pl.semaphore_wait(barrier, ctx_count - 1 + data_count - 1)

    @functools.partial(loop, me + 1, ctx_count)
    def _(rank):
        remote(
            st_all.at[me], st_all.at[me], st_send.at[rank], st_recv.at[me], ctx_at(rank)
        ).start()

    @functools.partial(loop, me + 1, ctx_count)
    def _(rank):
        remote(
            kv_all.at[me], kv_all.at[me], kv_send.at[rank], kv_recv.at[me], ctx_at(rank)
        ).start()

    lane = lax.broadcasted_iota(jnp.int32, (rows, LANES), 1)
    part = lane // head_dim

    def stack(values, target):
        for group in range(groups):
            block = values[:, group * LANES : (group + 1) * LANES]
            for index in range(per):
                target[group, index * rows : (index + 1) * rows, :] = jnp.where(
                    part == index, block, 0.0
                ).astype(BF16)

    def unstack(source):
        columns = []
        for group in range(groups):
            block = source[group, :rows, :]
            for index in range(1, per):
                block = jnp.where(
                    part == index, source[group, index * rows : (index + 1) * rows, :], block
                )
            columns.append(block)
        return jnp.concatenate(columns, axis=1)

    load_uq.wait()
    pre_uq = mul(rounded, wp[:, : 2 * att])
    pre_ref[:, : 2 * att] = pre_uq
    act_uq = pre_uq * sigmoid(pre_uq)
    gate_ref[...] = act_uq[:, :att].astype(BF16).astype(F32)
    stack(act_uq[:, att:] * score_scale, qs)
    load_go.wait()
    load_wo.wait()
    grad_gated = mul(go[...], wo[...], NT)

    chunk = 32

    @functools.partial(loop, 0, me + 1)
    def _(turn):
        block = me - turn

        @pl.when(turn > 0)
        def _():
            remote(
                st_all.at[block], st_all.at[block], st_send.at[block], st_recv.at[block],
                ctx_at(block),
            ).wait_recv()

        key_stamps = st_all[block][0:1, :]
        for first in range(0, rows, chunk):
            gap = scol[first : first + chunk, :] - key_stamps
            bucket = jnp.zeros(gap.shape, jnp.int32)
            bias = [jnp.full(gap.shape, steps[0, head], F32) for head in range(head_count)]
            for level in range(level_count - 1):
                above = gap >= (1 << level)
                bucket = jnp.where(above, level + 1, bucket)
                bias = [
                    jnp.where(above, steps[level + 1, head], bias[head])
                    for head in range(head_count)
                ]
            buckets[block, first : first + chunk, :] = bucket
            for head in range(head_count):
                start = (head % per) * rows + first
                sc[block, head // per, start : start + chunk, :] = bias[head]

    own_pos = me * rows + lax.broadcasted_iota(jnp.int32, (rows, LANES), 0)
    share = 1.0 / (jnp.minimum(own_pos, length - 1) + 1).astype(F32)
    mix[...] = jnp.zeros_like(mix)
    dq[...] = jnp.zeros_like(dq)

    @functools.partial(loop, 0, me + 1)
    def _(turn):
        block = me - turn

        @pl.when(turn > 0)
        def _():
            remote(
                kv_all.at[block], kv_all.at[block], kv_send.at[block], kv_recv.at[block],
                ctx_at(block),
            ).wait_recv()

        key_pos = block * rows + lane
        part_share = jnp.where((key_pos <= own_pos) & (key_pos < length), share, 0.0)
        shares = jnp.concatenate([part_share] * per, axis=0)
        for group in range(groups):
            keys = kv_all[block, :, group * LANES : (group + 1) * LANES]
            values = kv_all[block, :, att + group * LANES : att + (group + 1) * LANES]
            scores = mul(qs[group], keys, NT) + sc[block, group]
            sig = sigmoid(scores)
            shared = sig * shares
            weights = (scores * shared).astype(BF16)
            sc[block, group] = shared * (1.0 + scores * (1.0 - sig))
            wt[block, group] = weights
            mix[group] += mul(weights, values)

    mixed_norm, mixed_inv = norm_rows(unstack(mix))
    gate = gate_ref[...]
    grad_units = grad_gated * mixed_norm
    stack(norm_back(grad_gated * gate, mixed_norm, mixed_inv), gs)

    @functools.partial(loop, 0, me + 1)
    def _(block):
        for group in range(groups):
            low, high = group * LANES, (group + 1) * LANES
            keys = kv_all[block, :, low:high]
            values = kv_all[block, :, att + low : att + high]
            grad_scores = (mul(gs[group], values, NT) * sc[block, group]).astype(BF16)
            sc[block, group] = grad_scores.astype(F32)
            dq[group] += mul(grad_scores, keys)
            grad_k = mul(grad_scores, qs[group], TN)
            grad_val = mul(wt[block, group], gs[group], TN)
            own[:, low:high] = grad_k
            own[:, att + low : att + high] = grad_val
            snd[block, :, low:high] = grad_k.astype(BF16)
            snd[block, :, att + low : att + high] = grad_val.astype(BF16)

        @pl.when(block < me)
        def _():
            remote(
                snd.at[block], rcv.at[me], d_send.at[block], d_recv.at[me], ctx_at(block)
            ).start()

    tacc[...] = jnp.zeros_like(tacc)

    @functools.partial(loop, 0, me + 1)
    def _(block):
        bucket = buckets[block]
        for level in range(level_count):
            found = bucket == level
            for head in range(head_count):
                start = (head % per) * rows
                terms = jnp.where(found, sc[block, head // per, start : start + rows, :], 0.0)
                tacc[head, level] += jnp.sum(terms.reshape(rows // 8, 8, LANES), axis=0)

    table_lane = lax.broadcasted_iota(jnp.int32, (level_count, LANES), 1)
    local = jnp.zeros((level_count, LANES), F32)
    for head in range(head_count):
        summed = jnp.sum(jnp.sum(tacc[head], axis=1), axis=-1, keepdims=True)
        local = jnp.where(table_lane == head, summed, local)
    tab1[me] = local

    @functools.partial(loop, 1, ctx_count)
    def _(offset):
        rank = ctx_peer(offset)
        remote(
            tab1.at[me], tab1.at[me], t1_send.at[rank], t1_recv.at[me], ctx_at(rank)
        ).start()

    gated = (mixed_norm * gate).astype(BF16)
    layer_v[...] = (xv[...].astype(F32) + mul(gated, wo[...])).astype(BF16)
    write_layer = pltpu.make_async_copy(layer_v, layer_hbm, out_sem.at[0])
    write_layer.start()

    slope_uq = silu_slope(pre_ref[:, : 2 * att])
    grad_uq = jnp.concatenate([grad_units, unstack(dq) * score_scale], axis=1) * slope_uq
    grad_normed = mul(grad_uq.astype(BF16), wp[:, : 2 * att], NT)

    @functools.partial(loop, 1, ctx_count)
    def _(offset):
        rank = ctx_peer(offset)
        remote(
            tab1.at[rank], tab1.at[rank], t1_send.at[rank], t1_recv.at[rank], ctx_at(rank)
        ).wait_recv()

    group_sum = tab1[0]
    for rank in range(1, ctx_count):
        group_sum = group_sum + tab1[rank]
    tab2[my_dp] = group_sum

    @functools.partial(loop, 1, data_count)
    def _(offset):
        rank = dp_peer(offset)
        remote(
            tab2.at[my_dp], tab2.at[my_dp], t2_send.at[rank], t2_recv.at[my_dp], dp_at(rank)
        ).start()

    @functools.partial(loop, me + 1, ctx_count)
    def _(rank):
        remote(
            snd.at[rank], rcv.at[rank], d_send.at[rank], d_recv.at[rank], ctx_at(rank)
        ).wait_recv()
        own[...] += rcv[rank].astype(F32)

    grad_kv = own[...] * silu_slope(pre_ref[:, 2 * att :])
    grad_normed = grad_normed + mul(grad_kv.astype(BF16), wp[:, 2 * att :], NT)
    grad_v[...] = (
        norm_back(grad_normed, normed_ref[...], inverse) + go[...].astype(F32)
    ).astype(BF16)
    write_grad = pltpu.make_async_copy(grad_v, grad_hbm, out_sem.at[1])
    write_grad.start()

    @functools.partial(loop, 1, data_count)
    def _(offset):
        rank = dp_peer(offset)
        remote(
            tab2.at[rank], tab2.at[rank], t2_send.at[rank], t2_recv.at[rank], dp_at(rank)
        ).wait_recv()

    total = tab2[0]
    for rank in range(1, data_count):
        total = total + tab2[rank]
    gt_ref[...] = total[:, :head_count] * scale_table

    @functools.partial(loop, me + 1, ctx_count)
    def _(rank):
        remote(
            st_all.at[me], st_all.at[me], st_send.at[rank], st_recv.at[me], ctx_at(rank)
        ).wait_send()
        remote(
            kv_all.at[me], kv_all.at[me], kv_send.at[rank], kv_recv.at[me], ctx_at(rank)
        ).wait_send()

    @functools.partial(loop, 0, me)
    def _(block):
        remote(
            snd.at[block], rcv.at[me], d_send.at[block], d_recv.at[me], ctx_at(block)
        ).wait_send()

    @functools.partial(loop, 1, ctx_count)
    def _(offset):
        rank = ctx_peer(offset)
        remote(
            tab1.at[me], tab1.at[me], t1_send.at[rank], t1_recv.at[me], ctx_at(rank)
        ).wait_send()

    @functools.partial(loop, 1, data_count)
    def _(offset):
        rank = dp_peer(offset)
        remote(
            tab2.at[my_dp], tab2.at[my_dp], t2_send.at[rank], t2_recv.at[my_dp], dp_at(rank)
        ).wait_send()

    write_layer.wait()
    write_grad.wait()


def on_device(actions, stamps, lengths, w_proj, w_out, bias_table, grad_out):
    rows = actions.shape[1]
    model_dim = actions.shape[2]
    level_count, head_count = bias_table.shape
    att = w_out.shape[0]
    ctx_count = lax.axis_size("ctx")
    data_count = lax.axis_size("dp")
    groups = att // LANES
    per = LANES // (att // head_count)
    scale_table = 1.0 / math.sqrt(rows * ctx_count * data_count)
    vmem = pl.BlockSpec(memory_space=pltpu.VMEM)
    smem = pl.BlockSpec(memory_space=pltpu.SMEM)
    anywhere = pl.BlockSpec(memory_space=pl.ANY)
    dma = pltpu.SemaphoreType.DMA
    layer_rows, grad_rows, grad_table = pl.pallas_call(
        functools.partial(kernel, ctx_count, data_count, head_count, level_count, scale_table),
        out_shape=(
            jax.ShapeDtypeStruct((rows, model_dim), BF16),
            jax.ShapeDtypeStruct((rows, model_dim), BF16),
            jax.ShapeDtypeStruct((level_count, head_count), F32),
        ),
        in_specs=[smem, smem, vmem, anywhere, anywhere, anywhere, anywhere],
        out_specs=(anywhere, anywhere, vmem),
        scratch_shapes=[
            pltpu.VMEM((rows, model_dim), BF16),
            pltpu.VMEM((model_dim, 4 * att), BF16),
            pltpu.VMEM((att, model_dim), BF16),
            pltpu.VMEM((rows, model_dim), BF16),
            pltpu.VMEM((rows, model_dim), F32),
            pltpu.VMEM((rows, 4 * att), F32),
            pltpu.VMEM((rows, att), F32),
            pltpu.VMEM((ctx_count, rows, 2 * att), BF16),
            pltpu.VMEM((ctx_count, 8, LANES), jnp.int32),
            pltpu.VMEM((rows, LANES), jnp.int32),
            pltpu.SMEM((level_count, head_count), F32),
            pltpu.VMEM((groups, per * rows, LANES), BF16),
            pltpu.VMEM((groups, per * rows, LANES), BF16),
            pltpu.VMEM((ctx_count, rows, LANES), jnp.int32),
            pltpu.VMEM((ctx_count, groups, per * rows, LANES), F32),
            pltpu.VMEM((ctx_count, groups, per * rows, LANES), BF16),
            pltpu.VMEM((groups, per * rows, LANES), F32),
            pltpu.VMEM((groups, per * rows, LANES), F32),
            pltpu.VMEM((rows, 2 * att), F32),
            pltpu.VMEM((ctx_count, rows, 2 * att), BF16),
            pltpu.VMEM((ctx_count, rows, 2 * att), BF16),
            pltpu.VMEM((ctx_count, level_count, LANES), F32),
            pltpu.VMEM((data_count, level_count, LANES), F32),
            pltpu.VMEM((head_count, level_count, 8, LANES), F32),
            pltpu.VMEM((rows, model_dim), BF16),
            pltpu.VMEM((rows, model_dim), BF16),
            dma((5,)),
            dma((2,)),
            dma((ctx_count,)),
            dma((ctx_count,)),
            dma((ctx_count,)),
            dma((ctx_count,)),
            dma((ctx_count,)),
            dma((ctx_count,)),
            dma((ctx_count,)),
            dma((ctx_count,)),
            dma((data_count,)),
            dma((data_count,)),
        ],
        compiler_params=pltpu.CompilerParams(
            collective_id=0, has_side_effects=True, vmem_limit_bytes=48 * 1024 * 1024
        ),
    )(
        lengths,
        bias_table,
        stamps,
        actions.reshape(rows, model_dim),
        w_proj,
        w_out,
        grad_out.reshape(rows, model_dim),
    )
    return (
        layer_rows.reshape(1, rows, model_dim),
        grad_rows.reshape(1, rows, model_dim),
        grad_table,
    )


def solution(mesh):
    in_specs = (P("dp", "ctx", None), P("dp", "ctx"), P("dp"), P(), P(), P(), P("dp", "ctx", None))
    out_specs = (P("dp", "ctx", None), P("dp", "ctx", None), P())
    return jax.shard_map(
        on_device, mesh=mesh, in_specs=in_specs, out_specs=out_specs, check_vma=False
    )
```

time: 161 us -> 36.7 us (0.23)
  blocking collectives: 78.3 us -> 0 us
  local copies, waits for them, and re-layouts: 37.8 us -> 8 us
  matrix products: 29.7 us -> 0 us
  Pallas kernels: 0 us -> 27.1 us
  other arithmetic: 12.4 us -> 0 us
    psum x1 -> x0, blocking collectives: 39.8 us -> none  [on_device(): table_total = lax.psum(table_local, ('dp', 'ctx'))]
    all_gather x4 -> x0, blocking collectives: 38.5 us -> none  [the longest x1 10.5 us: on_device(): lax.all_gather(activated[:, 2 * attn_dim:], 'ctx', axis=0, tiled=True)]
    dot_general x11 -> x0, matrix products: 29.7 us -> none  [the longest x1 5.06 us: query_back_step(): jnp.einsum('qhd,khd->hqk', grad_heads, value_rows, preferred_element_type...]
    pallas_call x0 -> x1, Pallas kernels: none -> 27.1 us  [on_device(): pl.pallas_call(functools.partial(kernel, ctx_count, data_count, head_coun...]
    another operation x17 -> x0, local copies, waits for them, and re-layouts: 19.7 us -> none  [table_terms(): return jnp.stack(rows, axis=0)]
    slice x9 -> x0, local copies, waits for them, and re-layouts: 8.94 us -> none  [the longest x2 2.27 us: on_device(): own_values = activated[:, 3 * attn_dim:]]
    unnamed x54 -> x14, local copies, waits for them, and re-layouts: 0.68 us -> 8 us
    eq x1 -> x0, other arithmetic: 3.6 us -> none  [table_terms(): buckets[None] == level_index]
where the time goes in v1:
time: 36.7 us; the launch traced here: 36.4 us
  Pallas kernels  27.1 us (74%)
  local copies, waits for them, and re-layouts  8 us (22%)
  between operations  1.29 us (4%)
    pallas_call x1, Pallas kernels, on_device(): pl.pallas_call(functools.partial(kernel, ctx_count, data_count, head_coun...  27.1 us
    unnamed x14, local copies, waits for them, and re-layouts  8 us

profile of v1, /device:TPU:0, one launch (start us, length us, event | category | flops | bytes accessed | tf_op | source)
XLA Modules:
  0.0 36.4 jit_solution(9491564051439410201)
XLA Ops:
  1.3 0.8 %copy.10.table_ref = f32[16,4]{1,0:T(8,128)S(1)} copy(f32[16,4]{0,1:T(4,128)} %param.12) | data formatting | bytes 512 | tf_op args[5]
  2.0 0.0 copy-start
  2.0 1.6 %copy-done = bf16[1024,1024]{1,0:T(8,128)(2,1)S(1)} copy-done((bf16[1024,1024]{1,0:T(8,128)(2,1)S(1)}, bf16[1024,1024]{1,0:T(8,128)(2,1)}, u32[]{:S(2)}) %copy-start) | copy-done | bytes 2097176
  3.6 0.0 copy-start.1
  3.6 1.0 %copy-done.1 = bf16[256,1024]{1,0:T(8,128)(2,1)S(1)} copy-done((bf16[256,1024]{1,0:T(8,128)(2,1)S(1)}, bf16[256,1024]{1,0:T(8,128)(2,1)}, u32[]{:S(2)}) %copy-start.1) | copy-done | bytes 524312
  4.7 0.0 copy-start.2
  4.7 0.9 %copy-done.2 = bf16[1,128,1024]{2,1,0:T(8,128)(2,1)S(1)} copy-done((bf16[1,128,1024]{2,1,0:T(8,128)(2,1)S(1)}, bf16[1,128,1024]{2,1,0:T(8,128)(2,1)}, u32[]{:S(2)}) %copy-start.2) | copy-done | bytes 262168
  5.6 0.0 copy-start.3
  5.6 0.9 %copy-done.3 = bf16[1,128,1024]{2,1,0:T(8,128)(2,1)S(1)} copy-done((bf16[1,128,1024]{2,1,0:T(8,128)(2,1)S(1)}, bf16[1,128,1024]{2,1,0:T(8,128)(2,1)}, u32[]{:S(2)}) %copy-start.3) | copy-done | bytes 262168
  6.6 0.0 copy-start.4
  6.6 0.7 %copy-done.4 = s32[1,128]{1,0:T(1,128)S(1)} copy-done((s32[1,128]{1,0:T(1,128)S(1)}, s32[1,128]{1,0:T(1,128)}, u32[]{:S(2)}) %copy-start.4) | copy-done | bytes 536
  7.2 27.1 %shard_map.94 = (bf16[128,1024]{1,0:T(8,128)(2,1)S(1)}, bf16[128,1024]{1,0:T(8,128)(2,1)S(1)}, f32[16,4]{1,0:T(8,128)S(1)}) custom-call(s32[1]{0:T(128)S(6)} %copy.14.len_ref, f32[16,4]{1,0:T(8,128)S(1)} %copy.10.table_ref, s32[1,128]{1,0:T(1,128)S(1)} %copy-done.4, bf16[128,1024]{1,0:T(8,128)(2,1)S(1)} %bitcast.4, bf16[1024,1024]{1,0:T(8,128)(2,1)S(1)} %copy-done, ...), custom_call_target="tpu_custom_call" | custom-call | tf_op jit(solution)/shard_map/pallas_call | solution.py:392
  34.3 0.7 %copy.11 = f32[16,4]{0,1:T(4,128)} copy(f32[16,4]{1,0:T(8,128)S(1)} %get-tuple-element.11) | data formatting | bytes 512
  35.0 0.7 %copy.15 = bf16[1,128,1024]{2,1,0:T(8,128)(2,1)} copy(bf16[1,128,1024]{2,1,0:T(8,128)(2,1)S(1)} %bitcast.7) | data formatting | bytes 524288
  35.7 0.7 %copy.16 = bf16[1,128,1024]{2,1,0:T(8,128)(2,1)} copy(bf16[1,128,1024]{2,1,0:T(8,128)(2,1)S(1)} %bitcast.6) | data formatting | bytes 524288
Async XLA Ops:
  2.0 1.6 %copy-start = (bf16[1024,1024]{1,0:T(8,128)(2,1)S(1)}, bf16[1024,1024]{1,0:T(8,128)(2,1)}, u32[]{:S(2)}) copy-start(bf16[1024,1024]{1,0:T(8,128)(2,1)} %wp_hbm.1) | copy-start | bytes 6291460
  3.6 1.0 %copy-start.1 = (bf16[256,1024]{1,0:T(8,128)(2,1)S(1)}, bf16[256,1024]{1,0:T(8,128)(2,1)}, u32[]{:S(2)}) copy-start(bf16[256,1024]{1,0:T(8,128)(2,1)} %wo_hbm.1) | copy-start | bytes 1572868
  4.7 0.9 %copy-start.2 = (bf16[1,128,1024]{2,1,0:T(8,128)(2,1)S(1)}, bf16[1,128,1024]{2,1,0:T(8,128)(2,1)}, u32[]{:S(2)}) copy-start(bf16[1,128,1024]{2,1,0:T(8,128)(2,1)} %param.7) | copy-start | bytes 786436
  5.6 0.9 %copy-start.3 = (bf16[1,128,1024]{2,1,0:T(8,128)(2,1)S(1)}, bf16[1,128,1024]{2,1,0:T(8,128)(2,1)}, u32[]{:S(2)}) copy-start(bf16[1,128,1024]{2,1,0:T(8,128)(2,1)} %param.13) | copy-start | bytes 786436
  6.6 0.7 %copy-start.4 = (s32[1,128]{1,0:T(1,128)S(1)}, s32[1,128]{1,0:T(1,128)}, u32[]{:S(2)}) copy-start(s32[1,128]{1,0:T(1,128)} %stamps_ref.1) | copy-start | bytes 1540

commit v2 on v1

--- a/solution.py
+++ b/solution.py
@@ -47,12 +47,11 @@
 
 def kernel(
     ctx_count, data_count, head_count, level_count, scale_table,
-    len_ref, table_ref, stamps_ref, x_hbm, wp_hbm, wo_hbm, go_hbm,
-    layer_hbm, grad_hbm, gt_ref,
-    xv, wp, wo, go, normed_ref, pre_ref, gate_ref, kv_all, st_all, scol, steps,
+    len_ref, table_ref, stamps_hbm, x_hbm, wp_hbm, wo_hbm, go_hbm,
+    layer_v, grad_v, gt_ref,
+    stamps_ref, xv, wp, wo, go, normed_ref, pre_ref, gate_ref, kv_all, st_all, scol, steps,
     qs, gs, buckets, sc, wt, mix, dq, own, snd, rcv, tab1, tab2, tacc,
-    layer_v, grad_v,
-    load_sem, out_sem, st_send, st_recv, kv_send, kv_recv, d_send, d_recv,
+    load_sem, st_send, st_recv, kv_send, kv_recv, d_send, d_recv,
     t1_send, t1_recv, t2_send, t2_recv,
 ):
     rows, model_dim = xv.shape
@@ -88,7 +87,8 @@
     )
     load_go = pltpu.make_async_copy(go_hbm, go, load_sem.at[3])
     load_wo = pltpu.make_async_copy(wo_hbm, wo, load_sem.at[4])
-    for load in (load_x, load_kv, load_uq, load_go, load_wo):
+    load_st = pltpu.make_async_copy(stamps_hbm, stamps_ref, load_sem.at[5])
+    for load in (load_st, load_x, load_kv, load_uq, load_go, load_wo):
         load.start()
 
     barrier = pltpu.get_barrier_semaphore()
@@ -109,12 +109,13 @@
 
     length = len_ref[0]
     for head in range(head_count):
-        running = table_ref[0, head]
+        running = table_ref[head, 0]
         steps[0, head] = running
         for level in range(level_count - 1):
-            running = running + (table_ref[level + 1, head] - table_ref[level, head])
+            running = running + (table_ref[head, level + 1] - table_ref[head, level])
             steps[level + 1, head] = running
 
+    load_st.wait()
     stamp_row = stamps_ref[...]
     st_all[me] = jnp.broadcast_to(stamp_row, (8, LANES))
     scol[...] = jnp.broadcast_to(stamp_row, (rows, LANES)).T
@@ -273,11 +274,15 @@
                 terms = jnp.where(found, sc[block, head // per, start : start + rows, :], 0.0)
                 tacc[head, level] += jnp.sum(terms.reshape(rows // 8, 8, LANES), axis=0)
 
-    table_lane = lax.broadcasted_iota(jnp.int32, (level_count, LANES), 1)
-    local = jnp.zeros((level_count, LANES), F32)
-    for head in range(head_count):
-        summed = jnp.sum(jnp.sum(tacc[head], axis=1), axis=-1, keepdims=True)
-        local = jnp.where(table_lane == head, summed, local)
+    cells = head_count * level_count
+    summed = jnp.concatenate(
+        [
+            jnp.sum(tacc[...], axis=2).reshape(cells, LANES),
+            jnp.zeros((LANES - cells, LANES), F32),
+        ],
+        axis=0,
+    )
+    local = jnp.broadcast_to(jnp.sum(summed.T, axis=0, keepdims=True), (8, LANES))
     tab1[me] = local
 
     @functools.partial(loop, 1, ctx_count)
@@ -289,8 +294,6 @@
 
     gated = (mixed_norm * gate).astype(BF16)
     layer_v[...] = (xv[...].astype(F32) + mul(gated, wo[...])).astype(BF16)
-    write_layer = pltpu.make_async_copy(layer_v, layer_hbm, out_sem.at[0])
-    write_layer.start()
 
     slope_uq = silu_slope(pre_ref[:, : 2 * att])
     grad_uq = jnp.concatenate([grad_units, unstack(dq) * score_scale], axis=1) * slope_uq
@@ -327,8 +330,6 @@
     grad_v[...] = (
         norm_back(grad_normed, normed_ref[...], inverse) + go[...].astype(F32)
     ).astype(BF16)
-    write_grad = pltpu.make_async_copy(grad_v, grad_hbm, out_sem.at[1])
-    write_grad.start()
 
     @functools.partial(loop, 1, data_count)
     def _(offset):
@@ -340,7 +341,9 @@
     total = tab2[0]
     for rank in range(1, data_count):
         total = total + tab2[rank]
-    gt_ref[...] = total[:, :head_count] * scale_table
+    for head in range(head_count):
+        cells = total[0:1, head * level_count : (head + 1) * level_count]
+        gt_ref[head : head + 1, :] = cells * scale_table
 
     @functools.partial(loop, me + 1, ctx_count)
     def _(rank):
@@ -370,9 +373,6 @@
         remote(
             tab2.at[my_dp], tab2.at[my_dp], t2_send.at[rank], t2_recv.at[my_dp], dp_at(rank)
         ).wait_send()
-
-    write_layer.wait()
-    write_grad.wait()
 
 
 def on_device(actions, stamps, lengths, w_proj, w_out, bias_table, grad_out):
@@ -387,18 +387,19 @@
     scale_table = 1.0 / math.sqrt(rows * ctx_count * data_count)
     vmem = pl.BlockSpec(memory_space=pltpu.VMEM)
     smem = pl.BlockSpec(memory_space=pltpu.SMEM)
-    anywhere = pl.BlockSpec(memory_space=pl.ANY)
+    anywhere = pl.BlockSpec(memory_space=pltpu.HBM)
     dma = pltpu.SemaphoreType.DMA
     layer_rows, grad_rows, grad_table = pl.pallas_call(
         functools.partial(kernel, ctx_count, data_count, head_count, level_count, scale_table),
         out_shape=(
             jax.ShapeDtypeStruct((rows, model_dim), BF16),
             jax.ShapeDtypeStruct((rows, model_dim), BF16),
-            jax.ShapeDtypeStruct((level_count, head_count), F32),
+            jax.ShapeDtypeStruct((head_count, level_count), F32),
         ),
-        in_specs=[smem, smem, vmem, anywhere, anywhere, anywhere, anywhere],
-        out_specs=(anywhere, anywhere, vmem),
+        in_specs=[smem, smem, anywhere, anywhere, anywhere, anywhere, anywhere],
+        out_specs=(vmem, vmem, vmem),
         scratch_shapes=[
+            pltpu.VMEM((1, rows), jnp.int32),
             pltpu.VMEM((rows, model_dim), BF16),
             pltpu.VMEM((model_dim, 4 * att), BF16),
             pltpu.VMEM((att, model_dim), BF16),
@@ -420,13 +421,10 @@
             pltpu.VMEM((rows, 2 * att), F32),
             pltpu.VMEM((ctx_count, rows, 2 * att), BF16),
             pltpu.VMEM((ctx_count, rows, 2 * att), BF16),
-            pltpu.VMEM((ctx_count, level_count, LANES), F32),
-            pltpu.VMEM((data_count, level_count, LANES), F32),
+            pltpu.VMEM((ctx_count, 8, LANES), F32),
+            pltpu.VMEM((data_count, 8, LANES), F32),
             pltpu.VMEM((head_count, level_count, 8, LANES), F32),
-            pltpu.VMEM((rows, model_dim), BF16),
-            pltpu.VMEM((rows, model_dim), BF16),
-            dma((5,)),
-            dma((2,)),
+            dma((6,)),
             dma((ctx_count,)),
             dma((ctx_count,)),
             dma((ctx_count,)),
@@ -439,11 +437,11 @@
             dma((data_count,)),
         ],
         compiler_params=pltpu.CompilerParams(
-            collective_id=0, has_side_effects=True, vmem_limit_bytes=48 * 1024 * 1024
+            collective_id=0, has_side_effects=True, vmem_limit_bytes=60 * 1024 * 1024
         ),
     )(
         lengths,
-        bias_table,
+        bias_table.T,
         stamps,
         actions.reshape(rows, model_dim),
         w_proj,
@@ -453,7 +451,7 @@
     return (
         layer_rows.reshape(1, rows, model_dim),
         grad_rows.reshape(1, rows, model_dim),
-        grad_table,
+        grad_table.T,
     )
 
 

time: 36.7 us -> 33.5 us (0.913)
  local copies, waits for them, and re-layouts: 8 us -> 4.59 us
    unnamed x14 -> x3, local copies, waits for them, and re-layouts: 8 us -> 4.59 us
where the time goes in v2:
time: 33.5 us; the launch traced here: 33.2 us
  Pallas kernels  27.4 us (82%)
  local copies, waits for them, and re-layouts  4.59 us (14%)
  between operations  1.29 us (4%)
    pallas_call x1, Pallas kernels, on_device(): pl.pallas_call(functools.partial(kernel, ctx_count, data_count, head_coun...  27.4 us
    unnamed x3, local copies, waits for them, and re-layouts  4.59 us

profile of v2, /device:TPU:0, one launch (start us, length us, event | category | flops | bytes accessed | tf_op | source)
XLA Modules:
  0.0 33.2 jit_solution(4973205266275513105)
XLA Ops:
  1.3 27.4 %shard_map.94 = (bf16[128,1024]{1,0:T(8,128)(2,1)}, bf16[128,1024]{1,0:T(8,128)(2,1)}, f32[4,16]{1,0:T(4,128)}) custom-call(s32[1]{0:T(128)S(6)} %copy.13.len_ref, f32[4,16]{1,0:T(4,128)} %bitcast.10, s32[1,128]{1,0:T(1,128)} %stamps_hbm.1, bf16[128,1024]{1,0:T(8,128)(2,1)} %bitcast.6, bf16[1024,1024]{1,0:T(8,128)(2,1)} %wp_hbm.1, bf16[256,1024]{1,0:T(8,128)(2,1)} %wo_hbm.1, ...), custom_call_target="tpu_custom_call" | custom-call | tf_op jit(solution)/shard_map/pallas_call | solution.py:392
  28.7 1.7 %copy.14 = bf16[1,128,1024]{2,1,0:T(8,128)(2,1)} copy(bf16[1,128,1024]{2,1,0:T(8,128)(2,1)} %bitcast.9) | data formatting | bytes 524288
  30.3 1.7 %copy.15 = bf16[1,128,1024]{2,1,0:T(8,128)(2,1)} copy(bf16[1,128,1024]{2,1,0:T(8,128)(2,1)} %bitcast.8) | data formatting | bytes 524288
  32.0 1.3 %copy.16 = f32[16,4]{0,1:T(4,128)} copy(f32[16,4]{0,1:T(4,128)} %bitcast.11) | data formatting | bytes 512

commit v3 on v2

--- a/solution.py
+++ b/solution.py
@@ -48,10 +48,10 @@
 def kernel(
     ctx_count, data_count, head_count, level_count, scale_table,
     len_ref, table_ref, stamps_hbm, x_hbm, wp_hbm, wo_hbm, go_hbm,
-    layer_v, grad_v, gt_ref,
+    layer_hbm, grad_hbm, gt_ref,
     stamps_ref, xv, wp, wo, go, normed_ref, pre_ref, gate_ref, kv_all, st_all, scol, steps,
-    qs, gs, buckets, sc, wt, mix, dq, own, snd, rcv, tab1, tab2, tacc,
-    load_sem, st_send, st_recv, kv_send, kv_recv, d_send, d_recv,
+    q_all, g_all, qs, gs, buckets, sc, wt, mix, dq, own, tab1, tab2, tacc, layer_v, grad_v,
+    load_sem, out_sem, st_send, st_recv, kv_send, kv_recv, q_send, q_recv, g_send, g_recv,
     t1_send, t1_recv, t2_send, t2_recv,
 ):
     rows, model_dim = xv.shape
@@ -131,26 +131,27 @@
 
     pl.semaphore_wait(barrier, ctx_count - 1 + data_count - 1)
 
+    @functools.partial(loop, 1, ctx_count)
+    def _(offset):
+        rank = ctx_peer(offset)
+        remote(
+            st_all.at[me], st_all.at[me], st_send.at[rank], st_recv.at[me], ctx_at(rank)
+        ).start()
+
     @functools.partial(loop, me + 1, ctx_count)
     def _(rank):
         remote(
-            st_all.at[me], st_all.at[me], st_send.at[rank], st_recv.at[me], ctx_at(rank)
-        ).start()
-
-    @functools.partial(loop, me + 1, ctx_count)
-    def _(rank):
-        remote(
             kv_all.at[me], kv_all.at[me], kv_send.at[rank], kv_recv.at[me], ctx_at(rank)
         ).start()
 
     lane = lax.broadcasted_iota(jnp.int32, (rows, LANES), 1)
     part = lane // head_dim
 
-    def stack(values, target):
+    def stack(values, target, slot):
         for group in range(groups):
             block = values[:, group * LANES : (group + 1) * LANES]
             for index in range(per):
-                target[group, index * rows : (index + 1) * rows, :] = jnp.where(
+                target[slot, group, index * rows : (index + 1) * rows, :] = jnp.where(
                     part == index, block, 0.0
                 ).astype(BF16)
 
@@ -170,27 +171,25 @@
     pre_ref[:, : 2 * att] = pre_uq
     act_uq = pre_uq * sigmoid(pre_uq)
     gate_ref[...] = act_uq[:, :att].astype(BF16).astype(F32)
-    stack(act_uq[:, att:] * score_scale, qs)
+    own_q = act_uq[:, att:] * score_scale
+    q_all[me] = own_q.astype(BF16)
+
+    @functools.partial(loop, 0, me)
+    def _(rank):
+        remote(
+            q_all.at[me], q_all.at[me], q_send.at[rank], q_recv.at[me], ctx_at(rank)
+        ).start()
+
+    stack(own_q, qs, me)
     load_go.wait()
     load_wo.wait()
     grad_gated = mul(go[...], wo[...], NT)
 
     chunk = 32
 
-    @functools.partial(loop, 0, me + 1)
-    def _(turn):
-        block = me - turn
-
-        @pl.when(turn > 0)
-        def _():
-            remote(
-                st_all.at[block], st_all.at[block], st_send.at[block], st_recv.at[block],
-                ctx_at(block),
-            ).wait_recv()
-
-        key_stamps = st_all[block][0:1, :]
+    def add_bias(block, columns, key_stamps):
         for first in range(0, rows, chunk):
-            gap = scol[first : first + chunk, :] - key_stamps
+            gap = columns[first : first + chunk, :] - key_stamps
             bucket = jnp.zeros(gap.shape, jnp.int32)
             bias = [jnp.full(gap.shape, steps[0, head], F32) for head in range(head_count)]
             for level in range(level_count - 1):
@@ -205,8 +204,35 @@
                 start = (head % per) * rows + first
                 sc[block, head // per, start : start + chunk, :] = bias[head]
 
-    own_pos = me * rows + lax.broadcasted_iota(jnp.int32, (rows, LANES), 0)
-    share = 1.0 / (jnp.minimum(own_pos, length - 1) + 1).astype(F32)
+    def wait_stamps(rank):
+        remote(
+            st_all.at[rank], st_all.at[rank], st_send.at[rank], st_recv.at[rank], ctx_at(rank)
+        ).wait_recv()
+
+    @functools.partial(loop, 0, me + 1)
+    def _(turn):
+        block = me - turn
+
+        @pl.when(turn > 0)
+        def _():
+            wait_stamps(block)
+
+        add_bias(block, scol[...], st_all[block][0:1, :])
+
+    def score_block(block, query_at, first_query, first_key, keys_at):
+        query_pos = first_query * rows + lax.broadcasted_iota(jnp.int32, (rows, LANES), 0)
+        share = 1.0 / (jnp.minimum(query_pos, length - 1) + 1).astype(F32)
+        key_pos = first_key * rows + lane
+        part_share = jnp.where((key_pos <= query_pos) & (key_pos < length), share, 0.0)
+        shares = jnp.concatenate([part_share] * per, axis=0)
+        for group in range(groups):
+            keys = kv_all[keys_at, :, group * LANES : (group + 1) * LANES]
+            scores = mul(qs[query_at, group], keys, NT) + sc[block, group]
+            sig = sigmoid(scores)
+            shared = sig * shares
+            sc[block, group] = shared * (1.0 + scores * (1.0 - sig))
+            wt[block, group] = (scores * shared).astype(BF16)
+
     mix[...] = jnp.zeros_like(mix)
     dq[...] = jnp.zeros_like(dq)
 
@@ -221,46 +247,58 @@
                 ctx_at(block),
             ).wait_recv()
 
-        key_pos = block * rows + lane
-        part_share = jnp.where((key_pos <= own_pos) & (key_pos < length), share, 0.0)
-        shares = jnp.concatenate([part_share] * per, axis=0)
+        score_block(block, me, me, block, block)
         for group in range(groups):
-            keys = kv_all[block, :, group * LANES : (group + 1) * LANES]
             values = kv_all[block, :, att + group * LANES : att + (group + 1) * LANES]
-            scores = mul(qs[group], keys, NT) + sc[block, group]
-            sig = sigmoid(scores)
-            shared = sig * shares
-            weights = (scores * shared).astype(BF16)
-            sc[block, group] = shared * (1.0 + scores * (1.0 - sig))
-            wt[block, group] = weights
-            mix[group] += mul(weights, values)
+            mix[group] += mul(wt[block, group], values)
 
     mixed_norm, mixed_inv = norm_rows(unstack(mix))
     gate = gate_ref[...]
     grad_units = grad_gated * mixed_norm
-    stack(norm_back(grad_gated * gate, mixed_norm, mixed_inv), gs)
+    own_g = norm_back(grad_gated * gate, mixed_norm, mixed_inv)
+    g_all[me] = own_g.astype(BF16)
+
+    @functools.partial(loop, 0, me)
+    def _(rank):
+        remote(
+            g_all.at[me], g_all.at[me], g_send.at[rank], g_recv.at[me], ctx_at(rank)
+        ).start()
+
+    stack(own_g, gs, me)
+
+    @functools.partial(loop, me + 1, ctx_count)
+    def _(block):
+        wait_stamps(block)
+        stamp_block = jnp.broadcast_to(st_all[block][0:1, :], (rows, LANES))
+        add_bias(block, stamp_block.T, st_all[me][0:1, :])
+        remote(
+            q_all.at[block], q_all.at[block], q_send.at[block], q_recv.at[block], ctx_at(block)
+        ).wait_recv()
+        stack(q_all[block].astype(F32), qs, block)
+        score_block(block, block, block, me, me)
+
+    def back_scores(block, query_at, keys_at, group):
+        values = kv_all[keys_at, :, att + group * LANES : att + (group + 1) * LANES]
+        return (mul(gs[query_at, group], values, NT) * sc[block, group]).astype(BF16)
+
+    def add_key_grads(block, group, grad_scores):
+        low, high = group * LANES, (group + 1) * LANES
+        own[:, low:high] += mul(grad_scores, qs[block, group], TN)
+        own[:, att + low : att + high] += mul(wt[block, group], gs[block, group], TN)
+
+    own[...] = jnp.zeros_like(own)
 
     @functools.partial(loop, 0, me + 1)
     def _(block):
         for group in range(groups):
-            low, high = group * LANES, (group + 1) * LANES
-            keys = kv_all[block, :, low:high]
-            values = kv_all[block, :, att + low : att + high]
-            grad_scores = (mul(gs[group], values, NT) * sc[block, group]).astype(BF16)
+            keys = kv_all[block, :, group * LANES : (group + 1) * LANES]
+            grad_scores = back_scores(block, me, block, group)
             sc[block, group] = grad_scores.astype(F32)
             dq[group] += mul(grad_scores, keys)
-            grad_k = mul(grad_scores, qs[group], TN)
-            grad_val = mul(wt[block, group], gs[group], TN)
-            own[:, low:high] = grad_k
-            own[:, att + low : att + high] = grad_val
-            snd[block, :, low:high] = grad_k.astype(BF16)
-            snd[block, :, att + low : att + high] = grad_val.astype(BF16)
-
-        @pl.when(block < me)
-        def _():
-            remote(
-                snd.at[block], rcv.at[me], d_send.at[block], d_recv.at[me], ctx_at(block)
-            ).start()
+
+            @pl.when(block == me)
+            def _():
+                add_key_grads(block, group, grad_scores)
 
     tacc[...] = jnp.zeros_like(tacc)
 
@@ -294,6 +332,8 @@
 
     gated = (mixed_norm * gate).astype(BF16)
     layer_v[...] = (xv[...].astype(F32) + mul(gated, wo[...])).astype(BF16)
+    write_layer = pltpu.make_async_copy(layer_v, layer_hbm, out_sem.at[0])
+    write_layer.start()
 
     slope_uq = silu_slope(pre_ref[:, : 2 * att])
     grad_uq = jnp.concatenate([grad_units, unstack(dq) * score_scale], axis=1) * slope_uq
@@ -321,15 +361,19 @@
     @functools.partial(loop, me + 1, ctx_count)
     def _(rank):
         remote(
-            snd.at[rank], rcv.at[rank], d_send.at[rank], d_recv.at[rank], ctx_at(rank)
+            g_all.at[rank], g_all.at[rank], g_send.at[rank], g_recv.at[rank], ctx_at(rank)
         ).wait_recv()
-        own[...] += rcv[rank].astype(F32)
+        stack(g_all[rank].astype(F32), gs, rank)
+        for group in range(groups):
+            add_key_grads(rank, group, back_scores(rank, rank, me, group))
 
     grad_kv = own[...] * silu_slope(pre_ref[:, 2 * att :])
     grad_normed = grad_normed + mul(grad_kv.astype(BF16), wp[:, 2 * att :], NT)
     grad_v[...] = (
         norm_back(grad_normed, normed_ref[...], inverse) + go[...].astype(F32)
     ).astype(BF16)
+    write_grad = pltpu.make_async_copy(grad_v, grad_hbm, out_sem.at[1])
+    write_grad.start()
 
     @functools.partial(loop, 1, data_count)
     def _(offset):
@@ -348,24 +392,27 @@
     @functools.partial(loop, me + 1, ctx_count)
     def _(rank):
         remote(
+            kv_all.at[me], kv_all.at[me], kv_send.at[rank], kv_recv.at[me], ctx_at(rank)
+        ).wait_send()
+
+    @functools.partial(loop, 0, me)
+    def _(block):
+        remote(
+            q_all.at[me], q_all.at[me], q_send.at[block], q_recv.at[me], ctx_at(block)
+        ).wait_send()
+        remote(
+            g_all.at[me], g_all.at[me], g_send.at[block], g_recv.at[me], ctx_at(block)
+        ).wait_send()
+
+    @functools.partial(loop, 1, ctx_count)
+    def _(offset):
+        rank = ctx_peer(offset)
+        remote(
+            tab1.at[me], tab1.at[me], t1_send.at[rank], t1_recv.at[me], ctx_at(rank)
+        ).wait_send()
+        remote(
             st_all.at[me], st_all.at[me], st_send.at[rank], st_recv.at[me], ctx_at(rank)
         ).wait_send()
-        remote(
-            kv_all.at[me], kv_all.at[me], kv_send.at[rank], kv_recv.at[me], ctx_at(rank)
-        ).wait_send()
-
-    @functools.partial(loop, 0, me)
-    def _(block):
-        remote(
-            snd.at[block], rcv.at[me], d_send.at[block], d_recv.at[me], ctx_at(block)
-        ).wait_send()
-
-    @functools.partial(loop, 1, ctx_count)
-    def _(offset):
-        rank = ctx_peer(offset)
-        remote(
-            tab1.at[me], tab1.at[me], t1_send.at[rank], t1_recv.at[me], ctx_at(rank)
-        ).wait_send()
 
     @functools.partial(loop, 1, data_count)
     def _(offset):
@@ -373,6 +420,9 @@
         remote(
             tab2.at[my_dp], tab2.at[my_dp], t2_send.at[rank], t2_recv.at[my_dp], dp_at(rank)
         ).wait_send()
+
+    write_layer.wait()
+    write_grad.wait()
 
 
 def on_device(actions, stamps, lengths, w_proj, w_out, bias_table, grad_out):
@@ -397,7 +447,7 @@
             jax.ShapeDtypeStruct((head_count, level_count), F32),
         ),
         in_specs=[smem, smem, anywhere, anywhere, anywhere, anywhere, anywhere],
-        out_specs=(vmem, vmem, vmem),
+        out_specs=(anywhere, anywhere, vmem),
         scratch_shapes=[
             pltpu.VMEM((1, rows), jnp.int32),
             pltpu.VMEM((rows, model_dim), BF16),
@@ -411,20 +461,25 @@
             pltpu.VMEM((ctx_count, 8, LANES), jnp.int32),
             pltpu.VMEM((rows, LANES), jnp.int32),
             pltpu.SMEM((level_count, head_count), F32),
-            pltpu.VMEM((groups, per * rows, LANES), BF16),
-            pltpu.VMEM((groups, per * rows, LANES), BF16),
+            pltpu.VMEM((ctx_count, rows, att), BF16),
+            pltpu.VMEM((ctx_count, rows, att), BF16),
+            pltpu.VMEM((ctx_count, groups, per * rows, LANES), BF16),
+            pltpu.VMEM((ctx_count, groups, per * rows, LANES), BF16),
             pltpu.VMEM((ctx_count, rows, LANES), jnp.int32),
             pltpu.VMEM((ctx_count, groups, per * rows, LANES), F32),
             pltpu.VMEM((ctx_count, groups, per * rows, LANES), BF16),
             pltpu.VMEM((groups, per * rows, LANES), F32),
             pltpu.VMEM((groups, per * rows, LANES), F32),
             pltpu.VMEM((rows, 2 * att), F32),
-            pltpu.VMEM((ctx_count, rows, 2 * att), BF16),
-            pltpu.VMEM((ctx_count, rows, 2 * att), BF16),
             pltpu.VMEM((ctx_count, 8, LANES), F32),
             pltpu.VMEM((data_count, 8, LANES), F32),
             pltpu.VMEM((head_count, level_count, 8, LANES), F32),
+            pltpu.VMEM((rows, model_dim), BF16),
+            pltpu.VMEM((rows, model_dim), BF16),
             dma((6,)),
+            dma((2,)),
+            dma((ctx_count,)),
+            dma((ctx_count,)),
             dma((ctx_count,)),
             dma((ctx_count,)),
             dma((ctx_count,)),

time: 33.5 us -> 33 us (0.985)
  Pallas kernels: 27.4 us -> 26.9 us
    pallas_call x1, Pallas kernels: 27.4 us -> 26.9 us  [on_device(): pl.pallas_call(functools.partial(kernel, ctx_count, data_count, head_coun...]
where the time goes in v3:
time: 33 us; the launch traced here: 32.7 us
  Pallas kernels  26.9 us (82%)
  local copies, waits for them, and re-layouts  4.59 us (14%)
  between operations  1.29 us (4%)
    pallas_call x1, Pallas kernels, on_device(): pl.pallas_call(functools.partial(kernel, ctx_count, data_count, head_coun...  26.9 us
    unnamed x3, local copies, waits for them, and re-layouts  4.59 us

profile of v3, /device:TPU:0, one launch (start us, length us, event | category | flops | bytes accessed | tf_op | source)
XLA Modules:
  0.0 32.7 jit_solution(6274086694034441731)
XLA Ops:
  1.3 26.9 %shard_map.94 = (bf16[128,1024]{1,0:T(8,128)(2,1)}, bf16[128,1024]{1,0:T(8,128)(2,1)}, f32[4,16]{1,0:T(4,128)}) custom-call(s32[1]{0:T(128)S(6)} %copy.13.len_ref, f32[4,16]{1,0:T(4,128)} %bitcast.10, s32[1,128]{1,0:T(1,128)} %stamps_hbm.1, bf16[128,1024]{1,0:T(8,128)(2,1)} %bitcast.6, bf16[1024,1024]{1,0:T(8,128)(2,1)} %wp_hbm.1, bf16[256,1024]{1,0:T(8,128)(2,1)} %wo_hbm.1, ...), custom_call_target="tpu_custom_call" | custom-call | tf_op jit(solution)/shard_map/pallas_call | solution.py:442
  28.1 1.7 %copy.14 = bf16[1,128,1024]{2,1,0:T(8,128)(2,1)} copy(bf16[1,128,1024]{2,1,0:T(8,128)(2,1)} %bitcast.9) | data formatting | bytes 524288
  29.8 1.7 %copy.15 = bf16[1,128,1024]{2,1,0:T(8,128)(2,1)} copy(bf16[1,128,1024]{2,1,0:T(8,128)(2,1)} %bitcast.8) | data formatting | bytes 524288
  31.5 1.3 %copy.16 = f32[16,4]{0,1:T(4,128)} copy(f32[16,4]{0,1:T(4,128)} %bitcast.11) | data formatting | bytes 512

commit v4 on v3

--- a/solution.py
+++ b/solution.py
@@ -339,25 +339,6 @@
     grad_uq = jnp.concatenate([grad_units, unstack(dq) * score_scale], axis=1) * slope_uq
     grad_normed = mul(grad_uq.astype(BF16), wp[:, : 2 * att], NT)
 
-    @functools.partial(loop, 1, ctx_count)
-    def _(offset):
-        rank = ctx_peer(offset)
-        remote(
-            tab1.at[rank], tab1.at[rank], t1_send.at[rank], t1_recv.at[rank], ctx_at(rank)
-        ).wait_recv()
-
-    group_sum = tab1[0]
-    for rank in range(1, ctx_count):
-        group_sum = group_sum + tab1[rank]
-    tab2[my_dp] = group_sum
-
-    @functools.partial(loop, 1, data_count)
-    def _(offset):
-        rank = dp_peer(offset)
-        remote(
-            tab2.at[my_dp], tab2.at[my_dp], t2_send.at[rank], t2_recv.at[my_dp], dp_at(rank)
-        ).start()
-
     @functools.partial(loop, me + 1, ctx_count)
     def _(rank):
         remote(
@@ -366,6 +347,25 @@
         stack(g_all[rank].astype(F32), gs, rank)
         for group in range(groups):
             add_key_grads(rank, group, back_scores(rank, rank, me, group))
+
+    @functools.partial(loop, 1, ctx_count)
+    def _(offset):
+        rank = ctx_peer(offset)
+        remote(
+            tab1.at[rank], tab1.at[rank], t1_send.at[rank], t1_recv.at[rank], ctx_at(rank)
+        ).wait_recv()
+
+    group_sum = tab1[0]
+    for rank in range(1, ctx_count):
+        group_sum = group_sum + tab1[rank]
+    tab2[my_dp] = group_sum
+
+    @functools.partial(loop, 1, data_count)
+    def _(offset):
+        rank = dp_peer(offset)
+        remote(
+            tab2.at[my_dp], tab2.at[my_dp], t2_send.at[rank], t2_recv.at[my_dp], dp_at(rank)
+        ).start()
 
     grad_kv = own[...] * silu_slope(pre_ref[:, 2 * att :])
     grad_normed = grad_normed + mul(grad_kv.astype(BF16), wp[:, 2 * att :], NT)
@@ -423,6 +423,24 @@
 
     write_layer.wait()
     write_grad.wait()
+
+
+def hand_over(*refs):
+    count = len(refs) // 2
+    sems = refs[-1]
+    copies = []
+    for index in range(count):
+        source, target = refs[index], refs[count + index]
+        size = min(32, source.shape[0])
+        for first in range(0, source.shape[0], size):
+            part = pl.ds(first, size)
+            copies.append(
+                pltpu.make_async_copy(source.at[part], target.at[part], sems.at[len(copies)])
+            )
+    for copy in copies:
+        copy.start()
+    for copy in copies:
+        copy.wait()
 
 
 def on_device(actions, stamps, lengths, w_proj, w_out, bias_table, grad_out):
@@ -503,6 +521,15 @@
         w_out,
         grad_out.reshape(rows, model_dim),
     )
+    results = (layer_rows, grad_rows, grad_table)
+    layer_rows, grad_rows, grad_table = pl.pallas_call(
+        hand_over,
+        out_shape=tuple(jax.ShapeDtypeStruct(one.shape, one.dtype) for one in results),
+        in_specs=[anywhere] * 3,
+        out_specs=(anywhere,) * 3,
+        scratch_shapes=[dma((2 * (rows // 32) + 1,))],
+        compiler_params=pltpu.CompilerParams(vmem_limit_bytes=60 * 1024 * 1024),
+    )(*results)
     return (
         layer_rows.reshape(1, rows, model_dim),
         grad_rows.reshape(1, rows, model_dim),

time: 33 us -> 45.5 us (1.38)
  Pallas kernels: 26.9 us -> 44 us
  local copies, waits for them, and re-layouts: 4.59 us -> 0 us
    pallas_call x0 -> x1, Pallas kernels: none -> 17.1 us  [on_device(): pl.pallas_call(hand_over, out_shape=tuple((jax.ShapeDtypeStruct(one.shape...]
    unnamed x3 -> x0, local copies, waits for them, and re-layouts: 4.59 us -> none
where the time goes in v4:
time: 45.5 us; the launch traced here: 45.3 us
  Pallas kernels  44 us (97%)
  between operations  1.29 us (3%)
    pallas_call x1, Pallas kernels, on_device(): pl.pallas_call(functools.partial(kernel, ctx_count, data_count, head_coun...  26.9 us
    pallas_call x1, Pallas kernels, on_device(): pl.pallas_call(hand_over, out_shape=tuple((jax.ShapeDtypeStruct(one.shape...  17.1 us

profile of v4, /device:TPU:0, one launch (start us, length us, event | category | flops | bytes accessed | tf_op | source)
XLA Modules:
  0.0 45.3 jit_solution(376939608598230015)
XLA Ops:
  1.3 26.9 %shard_map.94 = (bf16[128,1024]{1,0:T(8,128)(2,1)}, bf16[128,1024]{1,0:T(8,128)(2,1)}, f32[4,16]{1,0:T(4,128)}) custom-call(s32[1]{0:T(128)S(6)} %copy.10.len_ref, f32[4,16]{1,0:T(4,128)} %bitcast.8, s32[1,128]{1,0:T(1,128)} %stamps_hbm.1, bf16[128,1024]{1,0:T(8,128)(2,1)} %bitcast.6, bf16[1024,1024]{1,0:T(8,128)(2,1)} %wp_hbm.1, bf16[256,1024]{1,0:T(8,128)(2,1)} %wo_hbm.1, ...), custom_call_target="tpu_custom_call" | custom-call | tf_op jit(solution)/shard_map/pallas_call | solution.py:460
  28.1 17.1 %shard_map.95 = (bf16[128,1024]{1,0:T(8,128)(2,1)}, bf16[128,1024]{1,0:T(8,128)(2,1)}, f32[4,16]{1,0:T(4,128)}) custom-call(bf16[128,1024]{1,0:T(8,128)(2,1)} %get-tuple-element.9.refs_0_, bf16[128,1024]{1,0:T(8,128)(2,1)} %get-tuple-element.10.refs_1_, f32[4,16]{1,0:T(4,128)} %get-tuple-element.11.refs_2_), custom_call_target="tpu_custom_call" | custom-call | tf_op jit(solution)/shard_map/pallas_call | solution.py:525

commit v5 on v4

--- a/solution.py
+++ b/solution.py
@@ -426,21 +426,26 @@
 
 
 def hand_over(*refs):
-    count = len(refs) // 2
-    sems = refs[-1]
-    copies = []
-    for index in range(count):
-        source, target = refs[index], refs[count + index]
-        size = min(32, source.shape[0])
+    sources, targets, held = refs[:3], refs[3:6], refs[6:9]
+    in_sems, out_sems = refs[9:]
+    loads, stores = [], []
+    for source, target, buffer in zip(sources, targets, held):
+        size = min(64, source.shape[0])
         for first in range(0, source.shape[0], size):
-            part = pl.ds(first, size)
-            copies.append(
-                pltpu.make_async_copy(source.at[part], target.at[part], sems.at[len(copies)])
+            part, index = pl.ds(first, size), len(loads)
+            loads.append(
+                pltpu.make_async_copy(source.at[part], buffer.at[part], in_sems.at[index])
             )
-    for copy in copies:
-        copy.start()
-    for copy in copies:
-        copy.wait()
+            stores.append(
+                pltpu.make_async_copy(buffer.at[part], target.at[part], out_sems.at[index])
+            )
+    for load in loads:
+        load.start()
+    for load, store in zip(loads, stores):
+        load.wait()
+        store.start()
+    for store in stores:
+        store.wait()
 
 
 def on_device(actions, stamps, lengths, w_proj, w_out, bias_table, grad_out):
@@ -527,7 +532,8 @@
         out_shape=tuple(jax.ShapeDtypeStruct(one.shape, one.dtype) for one in results),
         in_specs=[anywhere] * 3,
         out_specs=(anywhere,) * 3,
-        scratch_shapes=[dma((2 * (rows // 32) + 1,))],
+        scratch_shapes=[pltpu.VMEM(one.shape, one.dtype) for one in results]
+        + [dma((2 * (rows // 64) + 1,))] * 2,
         compiler_params=pltpu.CompilerParams(vmem_limit_bytes=60 * 1024 * 1024),
     )(*results)
     return (

time: 45.5 us -> 30.2 us (0.66)
  Pallas kernels: 44 us -> 28.7 us
    pallas_call x1, Pallas kernels: 17.1 us -> 1.84 us  [on_device(): pl.pallas_call(hand_over, out_shape=tuple((jax.ShapeDtypeStruct(one.shape...]
where the time goes in v5:
time: 30.2 us; the launch traced here: 30 us
  Pallas kernels  28.7 us (95%)
  between operations  1.29 us (4%)
    pallas_call x1, Pallas kernels, on_device(): pl.pallas_call(functools.partial(kernel, ctx_count, data_count, head_coun...  26.9 us
    pallas_call x1, Pallas kernels, on_device(): pl.pallas_call(hand_over, out_shape=tuple((jax.ShapeDtypeStruct(one.shape...  1.84 us

profile of v5, /device:TPU:0, one launch (start us, length us, event | category | flops | bytes accessed | tf_op | source)
XLA Modules:
  0.0 30.0 jit_solution(9083975392565341894)
XLA Ops:
  1.3 26.9 %shard_map.94 = (bf16[128,1024]{1,0:T(8,128)(2,1)}, bf16[128,1024]{1,0:T(8,128)(2,1)}, f32[4,16]{1,0:T(4,128)}) custom-call(s32[1]{0:T(128)S(6)} %copy.10.len_ref, f32[4,16]{1,0:T(4,128)} %bitcast.8, s32[1,128]{1,0:T(1,128)} %stamps_hbm.1, bf16[128,1024]{1,0:T(8,128)(2,1)} %bitcast.6, bf16[1024,1024]{1,0:T(8,128)(2,1)} %wp_hbm.1, bf16[256,1024]{1,0:T(8,128)(2,1)} %wo_hbm.1, ...), custom_call_target="tpu_custom_call" | custom-call | tf_op jit(solution)/shard_map/pallas_call | solution.py:465
  28.1 1.8 %shard_map.95 = (bf16[128,1024]{1,0:T(8,128)(2,1)}, bf16[128,1024]{1,0:T(8,128)(2,1)}, f32[4,16]{1,0:T(4,128)}) custom-call(bf16[128,1024]{1,0:T(8,128)(2,1)} %get-tuple-element.9.refs_0_, bf16[128,1024]{1,0:T(8,128)(2,1)} %get-tuple-element.10.refs_1_, f32[4,16]{1,0:T(4,128)} %get-tuple-element.11.refs_2_), custom_call_target="tpu_custom_call" | custom-call | tf_op jit(solution)/shard_map/pallas_call | solution.py:530

commit v6 on v5

--- a/solution.py
+++ b/solution.py
@@ -335,6 +335,7 @@
     write_layer = pltpu.make_async_copy(layer_v, layer_hbm, out_sem.at[0])
     write_layer.start()
 
+    pre_ref[:, 2 * att :] = silu_slope(pre_ref[:, 2 * att :])
     slope_uq = silu_slope(pre_ref[:, : 2 * att])
     grad_uq = jnp.concatenate([grad_units, unstack(dq) * score_scale], axis=1) * slope_uq
     grad_normed = mul(grad_uq.astype(BF16), wp[:, : 2 * att], NT)
@@ -367,7 +368,7 @@
             tab2.at[my_dp], tab2.at[my_dp], t2_send.at[rank], t2_recv.at[my_dp], dp_at(rank)
         ).start()
 
-    grad_kv = own[...] * silu_slope(pre_ref[:, 2 * att :])
+    grad_kv = own[...] * pre_ref[:, 2 * att :]
     grad_normed = grad_normed + mul(grad_kv.astype(BF16), wp[:, 2 * att :], NT)
     grad_v[...] = (
         norm_back(grad_normed, normed_ref[...], inverse) + go[...].astype(F32)

time: 30.2 us -> 30.2 us (level)
  no operation moved by 1% of the time
where the time goes in v6:
time: 30.2 us; the launch traced here: 30 us
  Pallas kernels  28.7 us (95%)
  between operations  1.29 us (4%)
    pallas_call x1, Pallas kernels, on_device(): pl.pallas_call(functools.partial(kernel, ctx_count, data_count, head_coun...  26.9 us
    pallas_call x1, Pallas kernels, on_device(): pl.pallas_call(hand_over, out_shape=tuple((jax.ShapeDtypeStruct(one.shape...  1.84 us

profile of v6, /device:TPU:0, one launch (start us, length us, event | category | flops | bytes accessed | tf_op | source)
XLA Modules:
  0.0 30.0 jit_solution(8745908931296777390)
XLA Ops:
  1.3 26.9 %shard_map.94 = (bf16[128,1024]{1,0:T(8,128)(2,1)}, bf16[128,1024]{1,0:T(8,128)(2,1)}, f32[4,16]{1,0:T(4,128)}) custom-call(s32[1]{0:T(128)S(6)} %copy.10.len_ref, f32[4,16]{1,0:T(4,128)} %bitcast.8, s32[1,128]{1,0:T(1,128)} %stamps_hbm.1, bf16[128,1024]{1,0:T(8,128)(2,1)} %bitcast.6, bf16[1024,1024]{1,0:T(8,128)(2,1)} %wp_hbm.1, bf16[256,1024]{1,0:T(8,128)(2,1)} %wo_hbm.1, ...), custom_call_target="tpu_custom_call" | custom-call | tf_op jit(solution)/shard_map/pallas_call | solution.py:466
  28.1 1.8 %shard_map.95 = (bf16[128,1024]{1,0:T(8,128)(2,1)}, bf16[128,1024]{1,0:T(8,128)(2,1)}, f32[4,16]{1,0:T(4,128)}) custom-call(bf16[128,1024]{1,0:T(8,128)(2,1)} %get-tuple-element.9.refs_0_, bf16[128,1024]{1,0:T(8,128)(2,1)} %get-tuple-element.10.refs_1_, f32[4,16]{1,0:T(4,128)} %get-tuple-element.11.refs_2_), custom_call_target="tpu_custom_call" | custom-call | tf_op jit(solution)/shard_map/pallas_call | solution.py:531
